TPU v7x, 32 devices: a whole 2x2x4 slice. The times are simulated.
32 devices in a mesh: cells: 2 (over x), pencil: 16 (over z, y, core).
Axes of the slice: x: 2, y: 2, z: 4, core: 2. Of those that a mesh axis runs over, the one named last changes fastest.
Arguments:
- multipoles: float32 [81, 128], P(None, ('cells', 'pencil')), parts along dimension 1, may hold values from -0.3 to 0.3
- positions: float32 [3, 128], P(None, ('cells', 'pencil')), parts along dimension 1, may hold values from 0 to 1
- species: int32 [128], P(('cells', 'pencil')), parts along dimension 0, may hold values from 0 to 2
- atom_slot: int32 [128], P('cells'), parts along dimension 0, may hold values from 0 to 63, each once
- pseudo_radial: float32 [3, 9, 262144], P(None, None, ('cells', 'pencil')), parts along dimension 2, may hold values from -1 to 1
- boundary_bessel: float32 [3, 9, 262144], P(None, None, ('cells', 'pencil')), parts along dimension 2, may hold values from -1 to 1
- interstitial: float32 [2, 262144], P(None, ('cells', 'pencil')), parts along dimension 1, may hold values from -6 to 6
- g_index: int32 [262144], P(('cells', 'pencil')), parts along dimension 0, may hold values from 0 to 1048575, as said below
Outputs:
- potential: float32 [512, 256, 256], P('cells', 'pencil'), parts along dimension 0
- boundary: float32 [81, 128], P(None, ('cells', 'pencil')), parts along dimension 1
There are 2 independent parts, one for each index of `cells`. A program takes and returns all parts, laid end to end along the dimension named above; each array names one. Nothing has to cross between parts.
Inputs may be any that keep to these rules, and one draw needn't show every extreme that they name: `g_index`: each block of 8192 entries belongs to one pencil index and holds distinct positions v of that index's 16 planes: plane v // 65536, row (v // 256) % 256, column v % 256. atom_slot is a permutation of the atoms. Atom a's inputs (multipoles, positions, species) are held by pencil index a // 4; its boundary values go to column atom_slot[a], which is held by pencil index atom_slot[a] // 4.
All inputs are finite; a program needn't handle non-finite values.
Results may differ from a plain program's by a relative error of at most 0.0003.
Values sent between devices are 32-bit elements; how exact they have to be, the bound alone decides.
No kernel may reach another device: no remote copies, remote signals or barrier semaphores. Data moves between devices by JAX's collectives and lax.ppermute only.
A program may use at most 128 MiB of HBM per device.

v0:
```python
import functools
import math

import jax
import jax.numpy as jnp
import numpy as np
from jax import lax
from jax.experimental import pallas as pl
from jax.experimental.pallas import tpu as pltpu
from jax.sharding import PartitionSpec as P

NG = 256
LMAX = 8
LM = 81
KINDS = 3
ROWS = 256
CHUNK = 1024
HIGH = lax.Precision.HIGHEST
TWO_PI = 2.0 * math.pi
F32 = jnp.float32
BF16 = jnp.bfloat16
I32 = jnp.int32
VMEM_BYTES = 56 * 1024 * 1024


def norm(degree, m_order):
    base = (
        (2 * degree + 1)
        / (4 * math.pi)
        * math.factorial(degree - m_order)
        / math.factorial(degree + m_order)
    )
    return math.sqrt(base) * (math.sqrt(2.0) if m_order else 1.0)


def table_layout():
    tile_rows = [(d, 0) for d in range(1, 9)]
    tile_rows += [(8, m) for m in range(1, 9)] + [(8, -m) for m in range(1, 9)]
    tile_rows += [(4, r + 1) if r < 4 else (4, -(8 - r)) for r in range(8)]
    for low in (1, 2, 3):
        for sign in (1, -1):
            tile_rows += [
                (low, sign * (r + 1)) if r < low else (8 - low, sign * (8 - r)) for r in range(8)
            ]
    rows = {}
    for kind in range(KINDS):
        for at, (degree, m_order) in enumerate(tile_rows):
            rows[kind * 88 + at] = (kind, degree, m_order)
    rows[80] = (0, 0, 0)
    rows[168] = (1, 0, 0)
    rows[81] = (2, 0, 0)
    return rows


def placement_tables():
    spread = np.zeros((KINDS, 128, ROWS), np.float32)
    even = np.zeros((KINDS, ROWS, 128), np.float32)
    odd = np.zeros((KINDS, ROWS, 128), np.float32)
    for row, (kind, degree, m_order) in table_layout().items():
        lm = degree * degree + degree + m_order
        spread[kind, lm, row] = 1.0
        sign = -1.0 if degree % 4 in (1, 2) else 1.0
        (even if degree % 2 == 0 else odd)[kind, row, lm] = sign
    return spread, np.concatenate([even, odd], 0)


def recurrence_table():
    out = np.zeros((8, 128), np.float64)
    for direction in range(2):
        for r in range(8):
            m = r + 1 if direction == 0 else 8 - r
            start = float(np.prod(np.arange(1, 2 * m, 2)))
            for degree in range(1, 9):
                at = 3 * (8 * direction + degree - 1)
                if degree == m:
                    out[r, at + 2] = start * norm(m, m)
                elif degree > m:
                    out[r, at] = (
                        (2 * degree - 1) / (degree - m) * norm(degree, m) / norm(degree - 1, m)
                    )
                    if degree > m + 1:
                        out[r, at + 1] = (
                            (degree + m - 1) / (degree - m) * norm(degree, m) / norm(degree - 2, m)
                        )
    return out.astype(np.float32)


def fit_even(values, count):
    x = np.cos(np.pi * (np.arange(400) + 0.5) / 400) * 0.125 + 0.125
    basis = np.polynomial.chebyshev.Chebyshev.fit(x, values(np.sqrt(x)), count - 1, domain=[0, 0.25])
    return [float(c) for c in basis.convert(kind=np.polynomial.Polynomial, domain=[-1, 1]).coef]


SIN_FIT = fit_even(lambda x: np.sin(np.pi * x) / x, 5)
COS_FIT = fit_even(lambda x: np.cos(np.pi * x), 5)


def horner(coefficients, x):
    total = coefficients[-1]
    for coefficient in coefficients[-2::-1]:
        total = total * x + coefficient
    return total


def turn(t):
    t = t - jnp.floor(t + 0.5)
    square = t * t
    half_sin = t * horner(SIN_FIT, square)
    half_cos = horner(COS_FIT, square)
    return 1.0 - 2.0 * half_sin * half_sin, 2.0 * half_sin * half_cos


def split(x):
    high = x.astype(BF16)
    return high, (x - high.astype(F32)).astype(BF16)


def signed(index):
    return jnp.where(index >= NG // 2, index - NG, index).astype(F32)


def frequencies(position, owner, count):
    jx = (position >> 16) * count + owner
    jy = (position >> 8) & 255
    jz = position & 255
    return jx, signed(jx), signed(jy), signed(jz)


def table_of(freq, radial_ref, coef_ref, rows_scratch):
    freq_x, freq_y, freq_z = freq
    size_sq = freq_x * freq_x + freq_y * freq_y + freq_z * freq_z
    inv_size = 1.0 / jnp.sqrt(jnp.maximum(size_sq, 1.0))
    unit_x, unit_y, unit_z = freq_x * inv_size, freq_y * inv_size, freq_z * inv_size
    radius_sq = unit_x * unit_x + unit_y * unit_y + unit_z * unit_z
    width = unit_x.shape[1]
    cosine, sine = unit_x, unit_y
    for m in range(1, 9):
        rows_scratch[0, m - 1 : m, :] = cosine
        rows_scratch[1, m - 1 : m, :] = sine
        rows_scratch[2, 8 - m : 9 - m, :] = cosine
        rows_scratch[3, 8 - m : 9 - m, :] = sine
        cosine, sine = cosine * unit_x - sine * unit_y, sine * unit_x + cosine * unit_y
    before, current = jnp.zeros_like(unit_z), jnp.ones_like(unit_z)
    for degree in range(1, 9):
        before, current = (
            current,
            (2 * degree - 1) / degree * unit_z * current
            - (degree - 1) / degree * radius_sq * before,
        )
        rows_scratch[4, degree - 1 : degree, :] = norm(degree, 0) * current
    wide_z = jnp.broadcast_to(unit_z, (8, width))
    wide_sq = jnp.broadcast_to(radius_sq, (8, width))
    plain = []
    for direction in range(2):
        before = jnp.zeros((8, width), F32)
        current = jnp.zeros((8, width), F32)
        by_degree = [None]
        for degree in range(1, 9 - direction):
            at = 3 * (8 * direction + degree - 1)
            following = coef_ref[:, at + 2 : at + 3] + (coef_ref[:, at : at + 1] * wide_z) * current
            if degree > 2:
                following = following - (coef_ref[:, at + 1 : at + 2] * wide_sq) * before
            before, current = current, following
            by_degree.append(current)
        plain.append(by_degree)
    forward, reverse = plain
    cos_f, sin_f, cos_r, sin_r = (rows_scratch[i] for i in range(4))
    sub = lax.broadcasted_iota(I32, (8, width), 0)
    harm = [rows_scratch[4], forward[8] * cos_f, forward[8] * sin_f]
    harm.append(jnp.where(sub < 4, forward[4] * cos_f, reverse[4] * sin_r))
    for low in (1, 2, 3):
        harm.append(jnp.where(sub < low, forward[low] * cos_f, reverse[8 - low] * cos_r))
        harm.append(jnp.where(sub < low, forward[low] * sin_f, reverse[8 - low] * sin_r))
    zeros = jnp.zeros((8, width), F32)
    pieces = []
    first = norm(0, 0)
    for kind in range(KINDS):
        line = [
            jnp.broadcast_to(radial_ref[d, kind : kind + 1, :], (8, width)) for d in range(1, 9)
        ]
        line = [None] + line
        for d in range(1, 9):
            rows_scratch[5 + kind, d - 1 : d, :] = radial_ref[d, kind : kind + 1, :]
        pieces.append(harm[0] * rows_scratch[5 + kind])
        pieces.append(harm[1] * line[8])
        pieces.append(harm[2] * line[8])
        pieces.append(harm[3] * line[4])
        for low in (1, 2, 3):
            both = jnp.where(sub < low, line[low], line[8 - low])
            pieces.append(harm[2 + 2 * low] * both)
            pieces.append(harm[3 + 2 * low] * both)
        if kind < 2:
            own = jnp.broadcast_to(radial_ref[0, kind : kind + 1, :], (8, width)) * first
            extra = jnp.where(sub == 0, own, zeros)
            if kind == 0:
                third = jnp.broadcast_to(radial_ref[0, 2:3, :], (8, width)) * first
                extra = jnp.where(sub == 1, third, extra)
            pieces.append(extra)
    return split(jnp.concatenate(pieces, 0))


def angles(atoms_ref, freq):
    freq_x, freq_y, freq_z = freq
    return turn(
        atoms_ref[:, LM : LM + 1] * freq_x
        + atoms_ref[:, LM + 1 : LM + 2] * freq_y
        + atoms_ref[:, LM + 2 : LM + 3] * freq_z
    )


def charge_kernel(
    count,
    place_ref,
    atoms_ref,
    spread_ref,
    coef_ref,
    radial_ref,
    inter_ref,
    index_ref,
    key_ref,
    order_ref,
    pot_ref,
    sent_ref,
    weights,
    rows_scratch,
    values,
):
    step = pl.program_id(0)
    atoms = atoms_ref.shape[0]
    per_chunk = CHUNK // 128

    @pl.when(step == 0)
    def _():
        kind = atoms_ref[:, LM + 3 : LM + 4]
        total = jnp.zeros((atoms, ROWS), F32)
        for s in range(KINDS):
            moved = jnp.dot(
                atoms_ref[...], spread_ref[s], precision=HIGH, preferred_element_type=F32
            )
            total = total + jnp.where(kind == float(s), moved, 0.0)
        high, low = split(total)
        weights[0:atoms, :] = high
        weights[atoms : 2 * atoms, :] = low

    jx, *freq = frequencies(index_ref[...], place_ref[0], count)
    table_high, table_low = table_of(freq, radial_ref, coef_ref, rows_scratch)
    main = jnp.dot(weights[...], table_high, preferred_element_type=F32)
    rest = jnp.dot(weights[0:atoms, :], table_low, preferred_element_type=F32)
    shape_part = main[0:atoms] + (main[atoms:] + rest)
    cosine, sine = angles(atoms_ref, freq)
    pseudo_re = jnp.sum(shape_part * cosine, axis=0, keepdims=True)
    pseudo_im = -jnp.sum(shape_part * sine, axis=0, keepdims=True)
    freq_x, freq_y, freq_z = freq
    size_sq = freq_x * freq_x + freq_y * freq_y + freq_z * freq_z
    kernel = jnp.where(size_sq > 0, 1.0 / jnp.maximum(size_sq, 1.0), 0.0)
    pot_re = (inter_ref[0:1, :] + pseudo_re) * kernel
    pot_im = (inter_ref[1:2, :] + pseudo_im) * kernel
    pot_ref[0:1, :] = pot_re
    pot_ref[1:2, :] = pot_im
    folded_im = jnp.where(jx > NG // 2, -pot_im, pot_im)
    for j in range(per_chunk):
        line = pl.ds(step * per_chunk + j, 1)
        values[0, line, :] = pot_re[:, j * 128 : (j + 1) * 128]
        values[1, line, :] = folded_im[:, j * 128 : (j + 1) * 128]

    @pl.when(step == pl.num_programs(0) - 1)
    def _():
        order = order_ref[...]
        lines = order.shape[0]
        lane = order & 127
        line_of = order >> 7

        def one_line(r, carried):
            taken_re, taken_im = carried
            here = line_of == r
            row_re = jnp.broadcast_to(values[0, pl.ds(r, 1), :], (lines, 128))
            row_im = jnp.broadcast_to(values[1, pl.ds(r, 1), :], (lines, 128))
            taken_re = jnp.where(here, jnp.take_along_axis(row_re, lane, axis=1), taken_re)
            taken_im = jnp.where(here, jnp.take_along_axis(row_im, lane, axis=1), taken_im)
            return taken_re, taken_im

        empty = jnp.zeros((lines, 128), F32)
        taken_re, taken_im = lax.fori_loop(0, lines, one_line, (empty, empty), unroll=8)
        key = key_ref[...]
        sent_ref[0:lines, :] = taken_re
        sent_ref[lines : 2 * lines, :] = taken_im
        sent_ref[2 * lines : 3 * lines, :] = key.astype(F32)
        at_lane = lax.broadcasted_iota(I32, (8, 128), 1)
        starts = jnp.zeros((8, 128), F32)
        for k in range(1, NG // count + 1):
            below = jnp.sum((key < (k << 16)).astype(F32), axis=(0, 1), keepdims=True)
            starts = jnp.where(at_lane == k, below, starts)
        sent_ref[3 * lines :, :] = starts


def boundary_kernel(
    count,
    place_ref,
    atoms_ref,
    gather_ref,
    coef_ref,
    slot_ref,
    bessel_ref,
    pot_ref,
    index_ref,
    out_ref,
    total,
    rows_scratch,
):
    step = pl.program_id(0)
    atoms = atoms_ref.shape[0]
    _, *freq = frequencies(index_ref[...], place_ref[0], count)
    table_high, table_low = table_of(freq, bessel_ref, coef_ref, rows_scratch)
    cosine, sine = angles(atoms_ref, freq)
    pot_re, pot_im = pot_ref[0:1, :], pot_ref[1:2, :]
    real_part = pot_re * cosine - pot_im * sine
    imag_part = pot_re * sine + pot_im * cosine
    high, low = split(jnp.concatenate([real_part, imag_part], 0))
    dims = (((1,), (1,)), ((), ()))
    both = lax.dot_general(
        jnp.concatenate([high, low], 0), table_high, dims, preferred_element_type=F32
    )
    rest = lax.dot_general(high, table_low, dims, preferred_element_type=F32)
    add = both[0 : 2 * atoms] + (both[2 * atoms :] + rest)

    @pl.when(step == 0)
    def _():
        total[...] = add

    @pl.when(step > 0)
    def _():
        total[...] += add

    @pl.when(step == pl.num_programs(0) - 1)
    def _():
        kind = atoms_ref[:, LM + 3 : LM + 4]
        raw = jnp.zeros((atoms, 128), F32)
        for s in range(KINDS):
            part = jnp.dot(
                total[0:atoms, :], gather_ref[s], precision=HIGH, preferred_element_type=F32
            ) + jnp.dot(
                total[atoms:, :], gather_ref[KINDS + s], precision=HIGH, preferred_element_type=F32
            )
            raw = raw + jnp.where(kind == float(s), part, 0.0)
        slots = lax.broadcasted_iota(I32, (atoms, atoms), 0)
        moved = (slots == slot_ref[...]).astype(F32)
        out_ref[...] = jnp.dot(moved, raw, precision=HIGH, preferred_element_type=F32)


def window_chunks(count, local_g):
    mean = local_g * count // NG
    return 2 * math.ceil((mean + 128 + 5 * math.sqrt(mean)) / 256)


def planes_kernel(count, pattern, finish, *refs):
    if finish:
        place_ref, start_ref, recv_ref, step_ref, wave_ref, before_ref, _ = refs[:7]
        own_ref, other_ref, box, front, back, spots, wave, earlier, sem = refs[7:]
    else:
        place_ref, start_ref, recv_ref, step_ref, box, front, back, spots = refs
    rows = NG // count
    planes = NG // count
    chip_rows = 2 * rows
    sources = recv_ref.shape[0]
    lines = (recv_ref.shape[1] - 8) // 3
    wide = window_chunks(count, lines * 128)
    half_planes = NG // 4
    per_plane = lines // planes
    place = place_ref[0]
    core = place % 2
    base = (place // 2) * chip_rows

    if finish and before_ref is not None:
        fetch = pltpu.make_async_copy(before_ref, earlier, sem)
        fetch.start()
    box[...] = jnp.zeros_like(box)
    for held in (front, back):
        held[lines:] = jnp.zeros((wide, 4 * chip_rows, 128), BF16)

    sub = lax.broadcasted_iota(I32, (8, 128), 0)
    if chip_rows == 8:
        start_rows = (base + (sub + core * rows) % chip_rows).astype(F32) * (1.0 / NG)
    else:
        start_rows = (base + core * rows + sub).astype(F32) * (1.0 / NG)
    across = (1 - 2 * core).astype(F32) * (rows / NG)

    def all_spots(s, _):
        keys = recv_ref[s, 2 * lines : 3 * lines, :].astype(I32)
        spots[s, 0:lines, :] = (((keys >> 16) << 8) | (keys & 255)).astype(F32)
        spots[s, lines:, :] = jnp.full((wide, 128), -1.0, F32)
        return 0

    lax.fori_loop(0, sources, all_spots, 0)

    def one_chunk(s, i, held):
        key = recv_ref[s, pl.ds(2 * lines + i, 1), :].astype(I32)
        v_re = recv_ref[s, pl.ds(i, 1), :]
        v_im = recv_ref[s, pl.ds(lines + i, 1), :]
        jy = ((key >> 8) & 255).astype(F32)
        wide_y = jnp.broadcast_to(jy, (8, 128))
        c, s = turn(wide_y * start_rows)
        parts = [(v_re * c - v_im * s, v_re * s + v_im * c)]
        if chip_rows > 8:
            c, s = turn(wide_y * (8.0 / NG))
            while 8 * len(parts) < rows:
                re, im = parts[-1]
                parts.append((re * c - im * s, re * s + im * c))
            c, s = turn(wide_y * across)
            parts += [(re * c - im * s, re * s + im * c) for re, im in parts]
        high, low = split(jnp.concatenate([re for re, _ in parts] + [im for _, im in parts], 0))
        held[i] = jnp.concatenate([high, low], 0)

    def start_of(s, k):
        return start_ref[s, 0, k].astype(I32)

    def one_window(s, k, first, held):
        left, right = [], []
        for j in range(wide):
            spot = spots[s, pl.ds(first + j, 1), :] - (k * NG).astype(F32)
            spot = jnp.broadcast_to(spot, (16, 128)).astype(BF16)
            hits = [
                jnp.where(
                    step_ref[16 * r : 16 * r + 16, :] == spot,
                    jnp.ones((16, 128), BF16),
                    jnp.zeros((16, 128), BF16),
                )
                for r in range(NG // 16)
            ]
            left.append(held[first + j])
            right.append(jnp.concatenate(hits, 0))
        out = lax.dot_general(
            jnp.concatenate(left, 1),
            jnp.concatenate(right, 1),
            (((1,), (1,)), ((), ())),
            preferred_element_type=F32,
        )
        owner = place ^ (4 * s + pattern) if pattern is not None else 2 * s + core
        jx = k * count + owner
        at = jnp.where(jx > NG // 2, NG - jx, jx) // 2
        box[at] += out[0 : 2 * chip_rows] + out[2 * chip_rows :]

    def one_source(s, held, following, filled):
        def one_plane(k, longest):
            first = start_of(s, k) // 128
            one_window(s, k, first, held)
            for j in range(per_plane):
                one_chunk(following, k * per_plane + j, filled)
            return jnp.maximum(longest, start_of(s, k + 1) - first * 128)

        unroll = 4 if planes % 4 == 0 and planes > 4 else 1
        longest = lax.fori_loop(0, planes, one_plane, jnp.int32(0), unroll=unroll)

        @pl.when(longest > wide * 128)
        def _():
            def long_plane(k, _):
                first = start_of(s, k) // 128
                more = (start_of(s, k + 1) - first * 128 + wide * 128 - 1) // (wide * 128)

                def again(j, _):
                    one_window(s, k, first + j * wide, held)
                    return 0

                return lax.fori_loop(1, more, again, 0)

            lax.fori_loop(0, planes, long_plane, 0)

    def first_chunks(g, _):
        for j in range(4):
            one_chunk(0, 4 * g + j, front)
        return 0

    lax.fori_loop(0, lines // 4, first_chunks, 0)

    def two_sources(t, _):
        one_source(2 * t, front, 2 * t + 1, back)
        one_source(2 * t + 1, back, jnp.minimum(2 * t + 2, sources - 1), front)
        return 0

    lax.fori_loop(0, sources // 2, two_sources, 0)
    if not finish:
        return

    wave[0], wave[1] = split(wave_ref[...])
    if before_ref is not None:
        fetch.wait()

    def along_z(at, number):
        size = number * 2 * chip_rows
        block = box[pl.ds(at, number)]
        if before_ref is not None:
            block = block + earlier[pl.ds(at, number)]
        high, low = split(block.reshape(size, NG))
        main = jnp.dot(jnp.concatenate([high, low], 0), wave[0], preferred_element_type=F32)
        rest = jnp.dot(high, wave[1], preferred_element_type=F32)
        full = (main[:size] + (main[size:] + rest)).reshape(number, 2 * chip_rows, 2 * NG)
        re, im = full[:, :chip_rows], full[:, chip_rows:]
        return re[:, :, :NG] - im[:, :, NG:], re[:, :, NG:] + im[:, :, :NG]

    def keep(at, value):
        line = pl.ds(at, rows, stride=NG // 2)
        for h in range(2):
            own_ref[h, line, :] = value[:rows, h * 128 : (h + 1) * 128]
            other_ref[h, line, :] = value[rows:, h * 128 : (h + 1) * 128]

    group = 4

    def some_planes(g, _):
        re, im = along_z(g * group, group)
        for j in range(group):
            keep(2 * (g * group + j), re[j])
            keep(2 * (g * group + j) + 1, im[j])
        return 0

    lax.fori_loop(0, half_planes // group, some_planes, 0, unroll=2)

    @pl.when(core == 0)
    def _():
        re, _ = along_z(half_planes, 1)
        keep(1, re[0])


def planes_call(count, place, recv, pattern, steps, finish=False, wave=None, before=None, after=None):
    rows = NG // count
    sources = recv.shape[0]
    lines = (recv.shape[1] - 8) // 3
    wide = window_chunks(count, lines * 128)
    half_rows = rows * NG // 2
    box = (NG // 4 + 1, 4 * rows, NG)
    vmem = pl.BlockSpec(memory_space=pltpu.VMEM)
    held = pltpu.VMEM((lines + wide, 8 * rows, 128), BF16)
    scratch = [held, held, pltpu.VMEM((sources, lines + wide, 128), F32)]
    start_spec = pl.BlockSpec(
        (sources, 8, 128), lambda i: (0, 3 * lines // 8, 0), memory_space=pltpu.SMEM
    )
    recv_spec = pl.BlockSpec(recv.shape, lambda i: (0, 0, 0))
    step_spec = pl.BlockSpec(steps.shape, lambda i: (0, 0))
    in_specs = [smem(), start_spec, recv_spec, step_spec]
    operands = [place, recv, recv, steps]
    kernel = functools.partial(planes_kernel, count, pattern, finish)
    if not finish:
        return pl.pallas_call(
            kernel,
            grid=(1,),
            in_specs=in_specs,
            out_specs=pl.BlockSpec(box, lambda i: (0, 0, 0)),
            out_shape=jax.ShapeDtypeStruct(box, F32),
            scratch_shapes=scratch,
            compiler_params=params(),
            name="planes_near",
        )(*operands)
    scratch = [pltpu.VMEM(box, F32)] + scratch + [pltpu.VMEM((2, NG, 2 * NG), BF16)]
    anywhere = pl.BlockSpec(memory_space=pl.ANY)
    in_specs.append(pl.BlockSpec(wave.shape, lambda i: (0, 0)))
    operands.append(wave)
    if before is None:
        inner = kernel
        at = len(in_specs)

        def kernel(*refs):
            inner(*refs[:at], None, *refs[at:], None, None)

    else:
        in_specs.append(anywhere)
        operands.append(before)
        scratch += [pltpu.VMEM(box, F32), pltpu.SemaphoreType.DMA]
    in_specs.append(anywhere)
    operands.append(after)
    return pl.pallas_call(
        kernel,
        grid=(1,),
        in_specs=in_specs,
        out_specs=[pl.BlockSpec((2, half_rows, 128), lambda i: (0, 0, 0))] * 2,
        out_shape=[jax.ShapeDtypeStruct((2, half_rows, 128), F32)] * 2,
        scratch_shapes=scratch,
        compiler_params=params(),
        name="planes",
    )(*operands)


def last_kernel(count, place_ref, own_ref, other_ref, wave_ref, _, out_ref, held, wave, sem):
    rows = NG // count
    half = NG // 2
    wave[0], wave[1] = split(wave_ref[place_ref[0] % 2])

    def one_row(y, _):
        line = pl.ds(pl.multiple_of(y * half, half), half)
        mixed = [
            jnp.concatenate([own_ref[h, line, :], other_ref[h, line, :]], 0) for h in range(2)
        ]
        high, low = split(jnp.concatenate(mixed, 1))
        main = jnp.dot(wave[...].reshape(2 * NG, NG), high, preferred_element_type=F32)
        rest = jnp.dot(wave[0], low, preferred_element_type=F32)
        out = main[:NG] + (main[NG:] + rest)
        for h in range(2):
            held[h, pl.ds(y, NG, stride=rows), :] = out[:, h * 128 : (h + 1) * 128]
        return 0

    lax.fori_loop(0, rows, one_row, 0, unroll=4)
    copies = [
        pltpu.make_async_copy(held.at[h], out_ref.at[:, pl.ds(h * 128, 128)], sem.at[h])
        for h in range(2)
    ]
    for copy in copies:
        copy.start()
    for copy in copies:
        copy.wait()


def wave_tables():
    j = np.arange(NG)
    phase = 2 * np.pi / NG * ((j[:, None] * j[None, :]) % NG)
    along_z = np.concatenate([np.cos(phase), np.sin(phase)], 1)
    classes = []
    for core in range(2):
        table = np.zeros((NG, NG // 2))
        for i in range(NG // 4):
            phase_x = 2 * np.pi / NG * ((j * (2 * i + core)) % NG)
            table[:, 2 * i] = np.cos(phase_x)
            table[:, 2 * i + 1] = -np.sin(phase_x)
        if core == 0:
            table[:, 1] = np.cos(np.pi * j)
        classes.append(table)
    along_x = [np.concatenate([classes[c], classes[1 - c]], 1) for c in range(2)]
    return along_z.astype(np.float32), np.stack(along_x).astype(np.float32)


def smem():
    return pl.BlockSpec(memory_space=pltpu.SMEM)


def params():
    return pltpu.CompilerParams(vmem_limit_bytes=VMEM_BYTES)


def body(
    multipoles, positions, species, atom_slot, pseudo_radial, boundary_bessel, interstitial, g_index
):
    count = lax.axis_size("pencil")
    owner = lax.axis_index("pencil").astype(I32)
    place = owner.reshape(1)
    local_g = g_index.shape[0]
    lines = local_g // 128
    chunks = local_g // CHUNK
    atoms = atom_slot.shape[0]
    own_atoms = multipoles.shape[1]
    rows = NG // count
    spread, gather = placement_tables()
    coef = jnp.asarray(recurrence_table())
    along_z, along_x = wave_tables()

    mine = jnp.concatenate(
        [multipoles, positions, species.astype(F32)[None, :], jnp.zeros((43, own_atoms), F32)], 0
    ).T
    copies = jnp.broadcast_to(mine[None], (count, own_atoms, 128))
    atom_rows = lax.all_to_all(copies, "pencil", split_axis=0, concat_axis=0, tiled=True)
    atom_rows = atom_rows.reshape(atoms, 128)

    jx = (g_index >> 16) * count + owner
    flip = jx > NG // 2
    jy = (g_index >> 8) & 255
    jz = g_index & 255
    folded = jnp.where(flip, ((-jy & 255) << 8) | (-jz & 255), (jy << 8) | jz)
    key, order = lax.sort(
        (((g_index >> 16) << 16) | folded, lax.iota(I32, local_g)), num_keys=1, is_stable=False
    )
    key = key.reshape(lines, 128)
    order = order.reshape(lines, 128)
    index_line = g_index.reshape(1, local_g)

    whole = lambda a: pl.BlockSpec(a.shape, lambda i: (0,) * a.ndim)
    line_spec = pl.BlockSpec((1, CHUNK), lambda i: (0, i))
    pair_spec = pl.BlockSpec((2, CHUNK), lambda i: (0, i))
    radial_spec = pl.BlockSpec((LMAX + 1, KINDS, CHUNK), lambda i: (0, 0, i))
    spread = jnp.asarray(spread)
    pot, sent = pl.pallas_call(
        functools.partial(charge_kernel, count),
        grid=(chunks,),
        in_specs=[
            smem(),
            whole(atom_rows),
            whole(spread),
            whole(coef),
            radial_spec,
            pair_spec,
            line_spec,
            whole(key),
            whole(order),
        ],
        out_specs=[pair_spec, pl.BlockSpec((3 * lines + 8, 128), lambda i: (0, 0))],
        out_shape=[
            jax.ShapeDtypeStruct((2, local_g), F32),
            jax.ShapeDtypeStruct((3 * lines + 8, 128), F32),
        ],
        scratch_shapes=[
            pltpu.VMEM((2 * atoms, ROWS), BF16),
            pltpu.VMEM((8, 8, CHUNK), F32),
            pltpu.VMEM((2, lines, 128), F32),
        ],
        compiler_params=params(),
        name="charge",
    )(place, atom_rows, spread, coef, pseudo_radial.transpose(1, 0, 2), interstitial, index_line, key, order)

    gather = jnp.asarray(gather)
    slot_line = atom_slot.reshape(1, atoms)
    partial_raw = pl.pallas_call(
        functools.partial(boundary_kernel, count),
        grid=(chunks,),
        in_specs=[
            smem(),
            whole(atom_rows),
            whole(gather),
            whole(coef),
            whole(slot_line),
            radial_spec,
            pair_spec,
            line_spec,
        ],
        out_specs=pl.BlockSpec((atoms, 128), lambda i: (0, 0)),
        out_shape=jax.ShapeDtypeStruct((atoms, 128), F32),
        scratch_shapes=[
            pltpu.VMEM((2 * atoms, ROWS), F32),
            pltpu.VMEM((8, 8, CHUNK), F32),
        ],
        compiler_params=params(),
        name="boundary",
    )(place, atom_rows, gather, coef, slot_line, boundary_bessel.transpose(1, 0, 2), pot, index_line)
    parts = lax.all_to_all(partial_raw, "pencil", split_axis=0, concat_axis=0, tiled=True)
    boundary = jnp.sum(parts.reshape(count, own_atoms, 128), axis=0)[:, :LM].T

    steps = jnp.asarray(np.broadcast_to(np.arange(NG)[:, None], (NG, 128)).astype(BF16))
    along_z = jnp.asarray(along_z)
    if count == 16:
        flipped = lambda bit: [(i, i ^ bit) for i in range(count)]
        near = jnp.stack(
            [sent] + [lax.ppermute(sent, "pencil", flipped(bit)) for bit in (4, 8, 12)]
        )
        far = lax.ppermute(near, "pencil", flipped(2))
        begun = planes_call(count, place, near, 0, steps)
        own, other = planes_call(
            count, place, far, 2, steps, True, along_z, begun, partial_raw
        )
    else:
        groups = [list(range(c, count, 2)) for c in range(2)]
        recv = lax.all_gather(sent, "pencil", axis_index_groups=groups)
        own, other = planes_call(
            count, place, recv, None, steps, True, along_z, None, partial_raw
        )
    other = lax.ppermute(other, "pencil", [(i, i ^ 1) for i in range(count)])

    vmem = pl.BlockSpec(memory_space=pltpu.VMEM)
    anywhere = pl.BlockSpec(memory_space=pl.ANY)
    potential = pl.pallas_call(
        functools.partial(last_kernel, count),
        in_specs=[smem(), vmem, vmem, vmem, anywhere],
        out_specs=anywhere,
        out_shape=jax.ShapeDtypeStruct((NG * rows, NG), F32),
        scratch_shapes=[
            pltpu.VMEM((2, NG * rows, 128), F32),
            pltpu.VMEM((2, NG, NG), BF16),
            pltpu.SemaphoreType.DMA((2,)),
        ],
        compiler_params=params(),
        name="last",
    )(place, own, other, jnp.asarray(along_x), parts)
    return (potential.reshape(NG, rows, NG), boundary)


def solution(mesh):
    placed = (
        P(None, ("cells", "pencil")),
        P(None, ("cells", "pencil")),
        P(("cells", "pencil")),
        P("cells"),
        P(None, None, ("cells", "pencil")),
        P(None, None, ("cells", "pencil")),
        P(None, ("cells", "pencil")),
        P(("cells", "pencil")),
    )
    return jax.shard_map(
        body,
        mesh=mesh,
        in_specs=placed,
        out_specs=(P("cells", "pencil", None), P(None, ("cells", "pencil"))),
        check_vma=False,
    )
```

profile of v0, /device:TPU:0, one launch (start us, length us, event | category | flops | bytes accessed | tf_op | source)
XLA Modules:
  0.0 124.9 jit_solution(1144618876226354988)
XLA Ops:
  0.6 0.7 convert_bitcast_fusion
  1.3 0.1 copy.17
  1.4 0.8 copy.16
  2.2 0.1 pad.7.clone
  2.2 0.8 maximum_bitcast_fusion
  3.0 0.6 broadcast_in_dim.14
  3.6 7.4 %all-to-all-start = ((f32[16,4,128]{2,1,0:T(4,128)}), f32[16,4,128]{2,1,0:T(4,128)S(1)}, u32[]{:S(2)}, u32[]{:S(2)}) async-start(f32[16,4,128]{2,1,0:T(4,128)} %broadcast_in_dim.14), calls=%async_computation | async-start | bytes 65536 | tf_op jit(solution)/shard_map/all_to_all | solution.py:655
  11.0 0.8 select_or_fusion
  11.8 6.3 %sort.15 = (s32[8192]{0:T(1024)}, s32[8192]{0:T(1024)}) sort(s32[8192]{0:T(1024)S(1)} %select_or_fusion, s32[8192]{0:T(1024)S(1)} %iota.3), dimensions={0}, to_apply=%region_0.1 | sort | flops 106496 | bytes 131072 | tf_op jit(solution)/shard_map/sort | solution.py:663
  18.1 0.0 all-to-all-done
  18.1 0.0 copy-start.5
  18.1 0.6 copy-done.5
  18.7 12.6 %charge.1 = (f32[2,8192]{1,0:T(2,128)}, f32[200,128]{1,0:T(8,128)}) custom-call(s32[1]{0:T(128)} %bitcast.place_ref.refs_0_, f32[64,128]{1,0:T(8,128)} %bitcast.28, f32[3,128,256]{2,1,0:T(8,128)} %constant.28.clone.spread_ref, f32[8,128]{1,0:T(8,128)} %constant.11.clone.coef_ref, f32[9,3,8192]{2,1,0:T(4,128)} %bitcast.22, f32[2,8192]{1,0:T(2,128)} %inter_ref.1, ...), custom_call_target="tpu_custom_call" | custom-call | tf_op jit(solution)/shard_map/charge/pallas_call | solution.py:675
  31.3 2.8 %collective-permute-start.1 = (f32[200,128]{1,0:T(8,128)}, f32[200,128]{1,0:T(8,128)S(1)}, u32[]{:S(2)}, u32[]{:S(2)}) collective-permute-start(f32[200,128]{1,0:T(8,128)} %get-tuple-element.10), channel_id=1, source_target_pairs={{0,8},{1,9},{2,10},{3,11},{4,12},{5,13},{6,14},{7,15},{8,0},{9,1},... | collective-permute-start | bytes 307208 | tf_op jit(solution)/shard_map/ppermute | solution.py:735
  34.1 1.5 %collective-permute-start.2 = (f32[200,128]{1,0:T(8,128)}, f32[200,128]{1,0:T(8,128)S(1)}, u32[]{:S(2)}, u32[]{:S(2)}) collective-permute-start(f32[200,128]{1,0:T(8,128)} %get-tuple-element.10), channel_id=1, source_target_pairs={{0,12},{1,13},{2,14},{3,15},{4,8},{5,9},{6,10},{7,11},{8,4},{9,5},... | collective-permute-start | bytes 307208 | tf_op jit(solution)/shard_map/ppermute | solution.py:735
  35.6 0.0 collective-permute-start
  35.6 6.9 %collective-permute-done.1 = f32[200,128]{1,0:T(8,128)S(1)} collective-permute-done((f32[200,128]{1,0:T(8,128)}, f32[200,128]{1,0:T(8,128)S(1)}, u32[]{:S(2)}, u32[]{:S(2)}) %collective-permute-start.1) | collective-permute-done | bytes 102432 | tf_op jit(solution)/shard_map/ppermute | solution.py:735
  42.5 0.0 collective-permute-done.2
  42.5 0.8 collective-permute-done
  43.4 0.9 pad_maximum_fusion.refs_1_.refs_2_
  44.3 0.0 copy-start
  44.3 1.7 %collective-permute-start.3 = (f32[4,200,128]{2,1,0:T(8,128)S(1)}, f32[4,200,128]{2,1,0:T(8,128)S(1)}, u32[]{:S(2)}, u32[]{:S(2)}) collective-permute-start(f32[4,200,128]{2,1,0:T(8,128)S(1)} %pad_maximum_fusion.refs_1_.refs_2_), channel_id=1, source_target_pairs={{0,2},{1,3},{2,0},{3,1},{4,6},{5,7},{6,4},{7,5},{8,10},{9,11},{10,... | collective-permute-start | bytes 1228808 | tf_op jit(solution)/shard_map/ppermute | solution.py:737
  46.0 10.3 %boundary.1.refs_6_ = f32[64,128]{1,0:T(8,128)} custom-call(s32[1]{0:T(128)} %bitcast.place_ref.refs_0_, f32[64,128]{1,0:T(8,128)} %bitcast.29, f32[6,256,128]{2,1,0:T(8,128)} %constant.29.clone.gather_ref, f32[8,128]{1,0:T(8,128)} %constant.11.clone.coef_ref, s32[1,64]{1,0:T(1,128)} %bitcast.36, f32[9,3,8192]{2,1,0:T(4,128)} %bitcast.23, ...), custom_call_target="tpu_custom_call" | custom-call | tf_op jit(solution)/shard_map/boundary/pallas_call | solution.py:705
  56.3 0.0 copy-done
  56.3 19.8 %planes_near.1.refs_5_ = f32[65,64,256]{2,1,0:T(8,128)} custom-call(s32[1]{0:T(128)} %bitcast.place_ref.refs_0_, f32[4,200,128]{2,1,0:T(8,128)} %copy-done, f32[4,200,128]{2,1,0:T(8,128)} %copy-done, bf16[256,128]{1,0:T(8,128)(2,1)} %constant.30.clone.refs_3_), custom_call_target="tpu_custom_call" | custom-call | tf_op jit(solution)/shard_map/planes_near/pallas_call | solution.py:541
  76.2 0.0 copy-start.3
  76.2 0.0 collective-permute-done.3.refs_1_.refs_2_
  76.2 0.0 copy-start.2
  76.2 0.8 copy-done.2
  77.0 27.4 %planes.1 = (f32[2,2048,128]{2,1,0:T(8,128)}, f32[2,2048,128]{2,1,0:T(8,128)}) custom-call(s32[1]{0:T(128)} %bitcast.place_ref.refs_0_, f32[4,200,128]{2,1,0:T(8,128)} %copy-done.2, f32[4,200,128]{2,1,0:T(8,128)} %copy-done.2, bf16[256,128]{1,0:T(8,128)(2,1)} %constant.30.clone.refs_3_, f32[256,512]{1,0:T(8,128)} %constant.31.clone.refs_4_, ...), custom_call_target="tpu_custom_call" | custom-call | tf_op jit(solution)/shard_map/planes/pallas_call | solution.py:568
  104.3 0.1 collective-permute-start.4
  104.4 0.0 copy-done.3
  104.4 11.2 %all_to_all.16 = f32[16,4,128]{2,1,0:T(4,128)S(1)} all-to-all(f32[16,4,128]{2,1,0:T(4,128)S(1)} %bitcast.24), channel_id=1, replica_groups=mesh['cells'=2,'pencil'=16] {'pencil'}, dimensions={0} | all-to-all | bytes 65536 | tf_op jit(solution)/shard_map/all_to_all | solution.py:727
  115.6 0.0 copy-start.4
  115.6 0.6 slice_bitcast_fusion
  116.2 0.0 collective-permute-done.4.other_ref
  116.2 0.0 copy-start.1
  116.2 0.0 copy-done.4
  116.2 1.3 %copy-done.1 = f32[2,2048,128]{2,1,0:T(8,128)} copy-done((f32[2,2048,128]{2,1,0:T(8,128)}, f32[2,2048,128]{2,1,0:T(8,128)S(1)}, u32[]{:S(2)}) %copy-start.1) | copy-done | bytes 2097176
  117.6 7.4 %last.1 = f32[4096,256]{1,0:T(8,128)} custom-call(s32[1]{0:T(128)} %bitcast.place_ref.refs_0_, f32[2,2048,128]{2,1,0:T(8,128)} %get-tuple-element.12.own_ref, f32[2,2048,128]{2,1,0:T(8,128)} %copy-done.1, f32[2,256,256]{2,1,0:T(8,128)} %constant.32.clone.wave_ref, f32[64,128]{1,0:T(8,128)} %bitcast.25), custom_call_target="tpu_custom_call" | custom-call | tf_op jit(solution)/shard_map/last/pallas_call | solution.py:752
  (3 shorter events, 0.0 us)
Async XLA Ops:
  3.6 14.5 %all-to-all-start = ((f32[16,4,128]{2,1,0:T(4,128)}), f32[16,4,128]{2,1,0:T(4,128)S(1)}, u32[]{:S(2)}, u32[]{:S(2)}) async-start(f32[16,4,128]{2,1,0:T(4,128)} %broadcast_in_dim.14), calls=%async_computation | async-start | bytes 65536 | tf_op jit(solution)/shard_map/all_to_all | solution.py:655
  18.1 0.6 copy-start.5
  31.3 11.2 %collective-permute-start.1 = (f32[200,128]{1,0:T(8,128)}, f32[200,128]{1,0:T(8,128)S(1)}, u32[]{:S(2)}, u32[]{:S(2)}) collective-permute-start(f32[200,128]{1,0:T(8,128)} %get-tuple-element.10), channel_id=1, source_target_pairs={{0,8},{1,9},{2,10},{3,11},{4,12},{5,13},{6,14},{7,15},{8,0},{9,1},... | collective-permute-start | bytes 307208 | tf_op jit(solution)/shard_map/ppermute | solution.py:735
  34.1 8.4 %collective-permute-start.2 = (f32[200,128]{1,0:T(8,128)}, f32[200,128]{1,0:T(8,128)S(1)}, u32[]{:S(2)}, u32[]{:S(2)}) collective-permute-start(f32[200,128]{1,0:T(8,128)} %get-tuple-element.10), channel_id=1, source_target_pairs={{0,12},{1,13},{2,14},{3,15},{4,8},{5,9},{6,10},{7,11},{8,4},{9,5},... | collective-permute-start | bytes 307208 | tf_op jit(solution)/shard_map/ppermute | solution.py:735
  35.6 7.8 %collective-permute-start = (f32[200,128]{1,0:T(8,128)}, f32[200,128]{1,0:T(8,128)S(1)}, u32[]{:S(2)}, u32[]{:S(2)}) collective-permute-start(f32[200,128]{1,0:T(8,128)} %get-tuple-element.10), channel_id=1, source_target_pairs={{0,4},{1,5},{2,6},{3,7},{4,0},{5,1},{6,2},{7,3},{8,12},{9,13},{10,... | collective-permute-start | bytes 307208 | tf_op jit(solution)/shard_map/ppermute | solution.py:735
  44.3 12.0 %copy-start = (f32[4,200,128]{2,1,0:T(8,128)}, f32[4,200,128]{2,1,0:T(8,128)S(1)}, u32[]{:S(2)}) copy-start(f32[4,200,128]{2,1,0:T(8,128)S(1)} %pad_maximum_fusion.refs_1_.refs_2_) | copy-start | bytes 1228804
  44.3 31.9 %collective-permute-start.3 = (f32[4,200,128]{2,1,0:T(8,128)S(1)}, f32[4,200,128]{2,1,0:T(8,128)S(1)}, u32[]{:S(2)}, u32[]{:S(2)}) collective-permute-start(f32[4,200,128]{2,1,0:T(8,128)S(1)} %pad_maximum_fusion.refs_1_.refs_2_), channel_id=1, source_target_pairs={{0,2},{1,3},{2,0},{3,1},{4,6},{5,7},{6,4},{7,5},{8,10},{9,11},{10,... | collective-permute-start | bytes 1228808 | tf_op jit(solution)/shard_map/ppermute | solution.py:737
  76.2 28.2 %copy-start.3 = (f32[64,128]{1,0:T(8,128)S(1)}, f32[64,128]{1,0:T(8,128)}, u32[]{:S(2)}) copy-start(f32[64,128]{1,0:T(8,128)} %boundary.1.refs_6_) | copy-start | bytes 98308
  76.2 0.8 copy-start.2
  104.3 11.9 %collective-permute-start.4 = (f32[2,2048,128]{2,1,0:T(8,128)}, f32[2,2048,128]{2,1,0:T(8,128)S(1)}, u32[]{:S(2)}, u32[]{:S(2)}) collective-permute-start(f32[2,2048,128]{2,1,0:T(8,128)} %get-tuple-element.13), channel_id=1, source_target_pairs={{0,1},{1,0},{2,3},{3,2},{4,5},{5,4},{6,7},{7,6},{8,9},{9,8},{10,11... | collective-permute-start | bytes 6291464 | tf_op jit(solution)/shard_map/ppermute | solution.py:748
  115.6 0.6 copy-start.4
  116.2 1.3 %copy-start.1 = (f32[2,2048,128]{2,1,0:T(8,128)}, f32[2,2048,128]{2,1,0:T(8,128)S(1)}, u32[]{:S(2)}) copy-start(f32[2,2048,128]{2,1,0:T(8,128)S(1)} %collective-permute-done.4.other_ref) | copy-start | bytes 6291460
where the time goes:
time: 126 us; the launch traced here: 125 us
  Pallas kernels  77.5 us (62%)
  starting transfers between devices  13.4 us (11%)
  blocking collectives  11.2 us (9%)
  other arithmetic  9.44 us (7%)
  waiting for transfers between devices  7.79 us (6%)
  local copies, waits for them, and re-layouts  4.88 us (4%)
    pallas_call x1, Pallas kernels, planes_call(): pl.pallas_call(kernel, grid=(1,), in_specs=in_specs, out_specs=[pl.BlockS...  27.4 us
    pallas_call x1, Pallas kernels, planes_call(): pl.pallas_call(kernel, grid=(1,), in_specs=in_specs, out_specs=pl.BlockSp...  19.8 us
    pallas_call x1, Pallas kernels, body(): pl.pallas_call(functools.partial(charge_kernel, count), grid=(chunks,), i...  12.6 us
    all_to_all x1, blocking collectives, body(): lax.all_to_all(partial_raw, 'pencil', split_axis=0, concat_axis=0, tiled=...  11.2 us
    pallas_call x1, Pallas kernels, body(): pl.pallas_call(functools.partial(boundary_kernel, count), grid=(chunks,),...  10.3 us
    ppermute x3, waiting for transfers between devices, body(): lax.ppermute(sent, 'pencil', flipped(bit))  7.79 us
    all_to_all x1, starting transfers between devices, body(): lax.all_to_all(copies, 'pencil', split_axis=0, concat_axis=0, tiled=True)  7.39 us
    pallas_call x1, Pallas kernels, body(): pl.pallas_call(functools.partial(last_kernel, count), in_specs=[smem(), v...  7.37 us
  transfers between devices with their start and end apart: 6, of which 2 were waited for; matrix products, arithmetic and copies ran while one was open for 6% of the time, Pallas kernels for 24%

commit v1 on v0

--- a/solution.py
+++ b/solution.py
@@ -14,7 +14,8 @@
 LM = 81
 KINDS = 3
 ROWS = 256
-CHUNK = 1024
+CHUNK = 2048
+PITCH = NG // 2 + 8
 HIGH = lax.Precision.HIGHEST
 TWO_PI = 2.0 * math.pi
 F32 = jnp.float32
@@ -208,6 +209,29 @@
     )
 
 
+def gather_kernel(
+    count, place_ref, moments_ref, positions_ref, species_ref, index_ref, out_ref, key_ref, held
+):
+    own = moments_ref.shape[0]
+    lane = lax.broadcasted_iota(I32, (own, 128), 1)
+    diagonal = lax.broadcasted_iota(I32, (own, own), 0) == lax.broadcasted_iota(I32, (own, own), 1)
+    total = jnp.zeros((own, 128), F32)
+    rows = [positions_ref[c : c + 1, :] for c in range(3)] + [species_ref[...].astype(F32)]
+    for c, row in enumerate(rows):
+        spread = jnp.where(diagonal, jnp.broadcast_to(row, (own, own)), 0.0)
+        column = jnp.sum(spread, axis=1, keepdims=True)
+        total = jnp.where(lane == LM + c, column, total)
+    held[...] = total
+    held[:, 0:LM] = moments_ref[...]
+    out_ref[...] = jnp.broadcast_to(held[...][None], out_ref.shape)
+    index = index_ref[...]
+    jx = (index >> 16) * count + place_ref[0]
+    jy = (index >> 8) & 255
+    jz = index & 255
+    folded = jnp.where(jx > NG // 2, ((-jy & 255) << 8) | (-jz & 255), (jy << 8) | jz)
+    key_ref[...] = ((index >> 16) << 16) | folded
+
+
 def charge_kernel(
     count,
     place_ref,
@@ -285,12 +309,16 @@
         sent_ref[0:lines, :] = taken_re
         sent_ref[lines : 2 * lines, :] = taken_im
         sent_ref[2 * lines : 3 * lines, :] = key.astype(F32)
-        at_lane = lax.broadcasted_iota(I32, (8, 128), 1)
-        starts = jnp.zeros((8, 128), F32)
-        for k in range(1, NG // count + 1):
+        begins = (lax.broadcasted_iota(I32, (8, 128), 1) * 256).astype(F32)
+        ends = begins + 255.0
+        first = jnp.zeros((8, 128), F32)
+        last = jnp.zeros((8, 128), F32)
+        for k in range(1, NG // count):
             below = jnp.sum((key < (k << 16)).astype(F32), axis=(0, 1), keepdims=True)
-            starts = jnp.where(at_lane == k, below, starts)
-        sent_ref[3 * lines :, :] = starts
+            first = first + jnp.where(below <= begins, 1.0, 0.0)
+            last = last + jnp.where(below <= ends, 1.0, 0.0)
+        sub = lax.broadcasted_iota(I32, (8, 128), 0)
+        sent_ref[3 * lines :, :] = jnp.where(sub == 0, first, last)
 
 
 def boundary_kernel(
@@ -347,25 +375,19 @@
         out_ref[...] = jnp.dot(moved, raw, precision=HIGH, preferred_element_type=F32)
 
 
-def window_chunks(count, local_g):
-    mean = local_g * count // NG
-    return 2 * math.ceil((mean + 128 + 5 * math.sqrt(mean)) / 256)
-
-
 def planes_kernel(count, pattern, finish, *refs):
     if finish:
         place_ref, start_ref, recv_ref, step_ref, wave_ref, before_ref, _ = refs[:7]
-        own_ref, other_ref, box, front, back, spots, wave, earlier, sem = refs[7:]
+        own_ref, other_ref, box, front, back, fields, wave, earlier, sem = refs[7:]
     else:
-        place_ref, start_ref, recv_ref, step_ref, box, front, back, spots = refs
+        place_ref, start_ref, recv_ref, step_ref, box, front, back, fields = refs
     rows = NG // count
-    planes = NG // count
     chip_rows = 2 * rows
     sources = recv_ref.shape[0]
     lines = (recv_ref.shape[1] - 8) // 3
-    wide = window_chunks(count, lines * 128)
     half_planes = NG // 4
-    per_plane = lines // planes
+    tiles = lines // 2
+    together = math.gcd(tiles, 16)
     place = place_ref[0]
     core = place % 2
     base = (place // 2) * chip_rows
@@ -374,8 +396,6 @@
         fetch = pltpu.make_async_copy(before_ref, earlier, sem)
         fetch.start()
     box[...] = jnp.zeros_like(box)
-    for held in (front, back):
-        held[lines:] = jnp.zeros((wide, 4 * chip_rows, 128), BF16)
 
     sub = lax.broadcasted_iota(I32, (8, 128), 0)
     if chip_rows == 8:
@@ -384,40 +404,48 @@
         start_rows = (base + core * rows + sub).astype(F32) * (1.0 / NG)
     across = (1 - 2 * core).astype(F32) * (rows / NG)
 
-    def all_spots(s, _):
+    def all_fields(s, _):
         keys = recv_ref[s, 2 * lines : 3 * lines, :].astype(I32)
-        spots[s, 0:lines, :] = (((keys >> 16) << 8) | (keys & 255)).astype(F32)
-        spots[s, lines:, :] = jnp.full((wide, 128), -1.0, F32)
+        jy = ((keys >> 8) & 255).astype(F32)
+        fields[s, 0] = jy
+        fields[s, 1] = (keys & 255).astype(F32)
+        fields[s, 2] = (keys >> 16).astype(F32)
+        if chip_rows > 8:
+            fields[s, 3], fields[s, 4] = turn(jy * (8.0 / NG))
+            fields[s, 5], fields[s, 6] = turn(jy * across)
         return 0
 
-    lax.fori_loop(0, sources, all_spots, 0)
+    lax.fori_loop(0, sources, all_fields, 0)
 
     def one_chunk(s, i, held):
-        key = recv_ref[s, pl.ds(2 * lines + i, 1), :].astype(I32)
         v_re = recv_ref[s, pl.ds(i, 1), :]
         v_im = recv_ref[s, pl.ds(lines + i, 1), :]
-        jy = ((key >> 8) & 255).astype(F32)
-        wide_y = jnp.broadcast_to(jy, (8, 128))
-        c, s = turn(wide_y * start_rows)
+        jy, c_step, s_step, c_far, s_far = (
+            fields[s, f, pl.ds(i, 1), :] if f == 0 or chip_rows > 8 else None
+            for f in (0, 3, 4, 5, 6)
+        )
+        c, s = turn(jnp.broadcast_to(jy, (8, 128)) * start_rows)
         parts = [(v_re * c - v_im * s, v_re * s + v_im * c)]
         if chip_rows > 8:
-            c, s = turn(wide_y * (8.0 / NG))
             while 8 * len(parts) < rows:
                 re, im = parts[-1]
-                parts.append((re * c - im * s, re * s + im * c))
-            c, s = turn(wide_y * across)
-            parts += [(re * c - im * s, re * s + im * c) for re, im in parts]
+                parts.append((re * c_step - im * s_step, re * s_step + im * c_step))
+            parts += [(re * c_far - im * s_far, re * s_far + im * c_far) for re, im in parts]
         high, low = split(jnp.concatenate([re for re, _ in parts] + [im for _, im in parts], 0))
         held[i] = jnp.concatenate([high, low], 0)
 
-    def start_of(s, k):
-        return start_ref[s, 0, k].astype(I32)
-
-    def one_window(s, k, first, held):
+    def edge(s, t, which):
+        return start_ref[s, which, t].astype(I32)
+
+    def plane_at(s, k):
+        owner = place ^ (4 * s + pattern) if pattern is not None else 2 * s + core
+        jx = k * count + owner
+        return jnp.where(jx > NG // 2, NG - jx, jx) // 2
+
+    def add_tile(s, t, wanted, held):
         left, right = [], []
-        for j in range(wide):
-            spot = spots[s, pl.ds(first + j, 1), :] - (k * NG).astype(F32)
-            spot = jnp.broadcast_to(spot, (16, 128)).astype(BF16)
+        for i in (2 * t, 2 * t + 1):
+            spot = jnp.broadcast_to(fields[s, 1, pl.ds(i, 1), :], (16, 128)).astype(BF16)
             hits = [
                 jnp.where(
                     step_ref[16 * r : 16 * r + 16, :] == spot,
@@ -426,50 +454,57 @@
                 )
                 for r in range(NG // 16)
             ]
-            left.append(held[first + j])
             right.append(jnp.concatenate(hits, 0))
+            plane = jnp.broadcast_to(fields[s, 2, pl.ds(i, 1), :], (16, 128))
+            phased = held[i]
+            masked = []
+            for k, used in wanted:
+                mask = jnp.where(plane == k.astype(F32), used, 0.0).astype(BF16)
+                masked.append(phased * jnp.concatenate([mask] * (phased.shape[0] // 16), 0))
+            left.append(jnp.concatenate(masked, 0))
         out = lax.dot_general(
             jnp.concatenate(left, 1),
             jnp.concatenate(right, 1),
             (((1,), (1,)), ((), ())),
             preferred_element_type=F32,
         )
-        owner = place ^ (4 * s + pattern) if pattern is not None else 2 * s + core
-        jx = k * count + owner
-        at = jnp.where(jx > NG // 2, NG - jx, jx) // 2
-        box[at] += out[0 : 2 * chip_rows] + out[2 * chip_rows :]
+        size = 2 * chip_rows
+        for j, (k, _) in enumerate(wanted):
+            box[plane_at(s, k)] += (
+                out[2 * j * size : (2 * j + 1) * size] + out[(2 * j + 1) * size : (2 * j + 2) * size]
+            )
 
     def one_source(s, held, following, filled):
-        def one_plane(k, longest):
-            first = start_of(s, k) // 128
-            one_window(s, k, first, held)
-            for j in range(per_plane):
-                one_chunk(following, k * per_plane + j, filled)
-            return jnp.maximum(longest, start_of(s, k + 1) - first * 128)
-
-        unroll = 4 if planes % 4 == 0 and planes > 4 else 1
-        longest = lax.fori_loop(0, planes, one_plane, jnp.int32(0), unroll=unroll)
-
-        @pl.when(longest > wide * 128)
+        def some_tiles(g, most):
+            for j in range(together):
+                t = g * together + j
+                first, last = edge(s, t, 0), edge(s, t, 1)
+                second = jnp.where(last > first, 1.0, 0.0)
+                add_tile(s, t, [(first, 1.0), (last, second)], held)
+                one_chunk(following, 2 * t, filled)
+                one_chunk(following, 2 * t + 1, filled)
+                most = jnp.maximum(most, last - first)
+            return most
+
+        most = lax.fori_loop(0, tiles // together, some_tiles, jnp.int32(0))
+
+        @pl.when(most > 1)
         def _():
-            def long_plane(k, _):
-                first = start_of(s, k) // 128
-                more = (start_of(s, k + 1) - first * 128 + wide * 128 - 1) // (wide * 128)
-
-                def again(j, _):
-                    one_window(s, k, first + j * wide, held)
+            def one_tile(t, _):
+                def between(k, _):
+                    add_tile(s, t, [(k, 1.0)], held)
                     return 0
 
-                return lax.fori_loop(1, more, again, 0)
-
-            lax.fori_loop(0, planes, long_plane, 0)
+                return lax.fori_loop(edge(s, t, 0) + 1, edge(s, t, 1), between, 0)
+
+            lax.fori_loop(0, tiles, one_tile, 0)
 
     def first_chunks(g, _):
-        for j in range(4):
-            one_chunk(0, 4 * g + j, front)
+        for j in range(8):
+            one_chunk(0, 8 * g + j, front)
         return 0
 
-    lax.fori_loop(0, lines // 4, first_chunks, 0)
+    lax.fori_loop(0, lines // 8, first_chunks, 0)
 
     def two_sources(t, _):
         one_source(2 * t, front, 2 * t + 1, back)
@@ -480,29 +515,33 @@
     if not finish:
         return
 
-    wave[0], wave[1] = split(wave_ref[...])
+    cos_z, sin_z = wave_ref[:, :NG], wave_ref[:, NG:]
+    for j, table in enumerate((wave_ref[...], jnp.concatenate([-sin_z, cos_z], 1))):
+        high, low = split(table)
+        for k, part in enumerate((high, high, low)):
+            wave[(3 * j + k) * NG : (3 * j + k + 1) * NG, :] = part
     if before_ref is not None:
         fetch.wait()
 
     def along_z(at, number):
-        size = number * 2 * chip_rows
         block = box[pl.ds(at, number)]
         if before_ref is not None:
             block = block + earlier[pl.ds(at, number)]
-        high, low = split(block.reshape(size, NG))
-        main = jnp.dot(jnp.concatenate([high, low], 0), wave[0], preferred_element_type=F32)
-        rest = jnp.dot(high, wave[1], preferred_element_type=F32)
-        full = (main[:size] + (main[size:] + rest)).reshape(number, 2 * chip_rows, 2 * NG)
-        re, im = full[:, :chip_rows], full[:, chip_rows:]
-        return re[:, :, :NG] - im[:, :, NG:], re[:, :, NG:] + im[:, :, :NG]
+        left = []
+        for part in (block[:, :chip_rows], block[:, chip_rows:]):
+            high, low = split(part.reshape(number * chip_rows, NG))
+            left += [high, low, high]
+        out = jnp.dot(jnp.concatenate(left, 1), wave[...], preferred_element_type=F32)
+        out = out.reshape(number, chip_rows, 2 * NG)
+        return out[:, :, :NG], out[:, :, NG:]
 
     def keep(at, value):
-        line = pl.ds(at, rows, stride=NG // 2)
+        line = pl.ds(at, rows, stride=PITCH)
         for h in range(2):
             own_ref[h, line, :] = value[:rows, h * 128 : (h + 1) * 128]
             other_ref[h, line, :] = value[rows:, h * 128 : (h + 1) * 128]
 
-    group = 4
+    group = 16
 
     def some_planes(g, _):
         re, im = along_z(g * group, group)
@@ -523,12 +562,11 @@
     rows = NG // count
     sources = recv.shape[0]
     lines = (recv.shape[1] - 8) // 3
-    wide = window_chunks(count, lines * 128)
-    half_rows = rows * NG // 2
+    half_rows = rows * PITCH
     box = (NG // 4 + 1, 4 * rows, NG)
     vmem = pl.BlockSpec(memory_space=pltpu.VMEM)
-    held = pltpu.VMEM((lines + wide, 8 * rows, 128), BF16)
-    scratch = [held, held, pltpu.VMEM((sources, lines + wide, 128), F32)]
+    held = pltpu.VMEM((lines, 8 * rows, 128), BF16)
+    scratch = [held, held, pltpu.VMEM((sources, 7, lines, 128), F32)]
     start_spec = pl.BlockSpec(
         (sources, 8, 128), lambda i: (0, 3 * lines // 8, 0), memory_space=pltpu.SMEM
     )
@@ -547,8 +585,9 @@
             scratch_shapes=scratch,
             compiler_params=params(),
             name="planes_near",
+        cost_estimate=cost(15),
         )(*operands)
-    scratch = [pltpu.VMEM(box, F32)] + scratch + [pltpu.VMEM((2, NG, 2 * NG), BF16)]
+    scratch = [pltpu.VMEM(box, F32)] + scratch + [pltpu.VMEM((6 * NG, 2 * NG), BF16)]
     anywhere = pl.BlockSpec(memory_space=pl.ANY)
     in_specs.append(pl.BlockSpec(wave.shape, lambda i: (0, 0)))
     operands.append(wave)
@@ -574,16 +613,16 @@
         scratch_shapes=scratch,
         compiler_params=params(),
         name="planes",
+        cost_estimate=cost(25),
     )(*operands)
 
 
 def last_kernel(count, place_ref, own_ref, other_ref, wave_ref, _, out_ref, held, wave, sem):
     rows = NG // count
-    half = NG // 2
     wave[0], wave[1] = split(wave_ref[place_ref[0] % 2])
 
     def one_row(y, _):
-        line = pl.ds(pl.multiple_of(y * half, half), half)
+        line = pl.ds(pl.multiple_of(y * PITCH, 8), NG // 2)
         mixed = [
             jnp.concatenate([own_ref[h, line, :], other_ref[h, line, :]], 0) for h in range(2)
         ]
@@ -628,6 +667,10 @@
     return pl.BlockSpec(memory_space=pltpu.SMEM)
 
 
+def cost(micros):
+    return pl.CostEstimate(flops=int(micros * 1e9), bytes_accessed=0, transcendentals=0)
+
+
 def params():
     return pltpu.CompilerParams(vmem_limit_bytes=VMEM_BYTES)
 
@@ -648,20 +691,30 @@
     coef = jnp.asarray(recurrence_table())
     along_z, along_x = wave_tables()
 
-    mine = jnp.concatenate(
-        [multipoles, positions, species.astype(F32)[None, :], jnp.zeros((43, own_atoms), F32)], 0
-    ).T
-    copies = jnp.broadcast_to(mine[None], (count, own_atoms, 128))
+    vmem = pl.BlockSpec(memory_space=pltpu.VMEM)
+    copies, key = pl.pallas_call(
+        functools.partial(gather_kernel, count),
+        in_specs=[smem(), vmem, vmem, vmem, vmem],
+        out_specs=[vmem, vmem],
+        out_shape=[
+            jax.ShapeDtypeStruct((count, own_atoms, 128), F32),
+            jax.ShapeDtypeStruct((lines, 128), I32),
+        ],
+        scratch_shapes=[pltpu.VMEM((own_atoms, 128), F32)],
+        compiler_params=params(),
+        name="atoms",
+    )(
+        place,
+        multipoles.T,
+        positions,
+        species.reshape(1, own_atoms),
+        g_index.reshape(lines, 128),
+    )
     atom_rows = lax.all_to_all(copies, "pencil", split_axis=0, concat_axis=0, tiled=True)
     atom_rows = atom_rows.reshape(atoms, 128)
 
-    jx = (g_index >> 16) * count + owner
-    flip = jx > NG // 2
-    jy = (g_index >> 8) & 255
-    jz = g_index & 255
-    folded = jnp.where(flip, ((-jy & 255) << 8) | (-jz & 255), (jy << 8) | jz)
     key, order = lax.sort(
-        (((g_index >> 16) << 16) | folded, lax.iota(I32, local_g)), num_keys=1, is_stable=False
+        (key.reshape(local_g), lax.iota(I32, local_g)), num_keys=1, is_stable=False
     )
     key = key.reshape(lines, 128)
     order = order.reshape(lines, 128)
@@ -698,6 +751,7 @@
         ],
         compiler_params=params(),
         name="charge",
+        cost_estimate=cost(10),
     )(place, atom_rows, spread, coef, pseudo_radial.transpose(1, 0, 2), interstitial, index_line, key, order)
 
     gather = jnp.asarray(gather)
@@ -723,6 +777,7 @@
         ],
         compiler_params=params(),
         name="boundary",
+        cost_estimate=cost(10),
     )(place, atom_rows, gather, coef, slot_line, boundary_bessel.transpose(1, 0, 2), pot, index_line)
     parts = lax.all_to_all(partial_raw, "pencil", split_axis=0, concat_axis=0, tiled=True)
     boundary = jnp.sum(parts.reshape(count, own_atoms, 128), axis=0)[:, :LM].T
@@ -731,13 +786,13 @@
     along_z = jnp.asarray(along_z)
     if count == 16:
         flipped = lambda bit: [(i, i ^ bit) for i in range(count)]
-        near = jnp.stack(
-            [sent] + [lax.ppermute(sent, "pencil", flipped(bit)) for bit in (4, 8, 12)]
-        )
+        pieces = [lax.ppermute(sent, "pencil", flipped(bit)) for bit in (4, 8, 12)]
+        pieces, partial_raw = lax.optimization_barrier((pieces, partial_raw))
+        near = jnp.stack([sent] + pieces)
         far = lax.ppermute(near, "pencil", flipped(2))
         begun = planes_call(count, place, near, 0, steps)
         own, other = planes_call(
-            count, place, far, 2, steps, True, along_z, begun, partial_raw
+            count, place, far, 2, steps, True, along_z, begun, parts
         )
     else:
         groups = [list(range(c, count, 2)) for c in range(2)]
@@ -761,6 +816,7 @@
         ],
         compiler_params=params(),
         name="last",
+        cost_estimate=cost(7),
     )(place, own, other, jnp.asarray(along_x), parts)
     return (potential.reshape(NG, rows, NG), boundary)
 

time: 126 us -> 98.1 us (0.78)
  Pallas kernels: 77.5 us -> 62.4 us
  blocking collectives: 11.2 us -> 0 us
  starting transfers between devices: 13.4 us -> 19.8 us
  waiting for transfers between devices: 7.79 us -> 3.19 us
  other arithmetic: 9.44 us -> 7.89 us
  local copies, waits for them, and re-layouts: 4.88 us -> 3.34 us
    all_to_all x1 -> x0, blocking collectives: 11.2 us -> none  [body(): lax.all_to_all(partial_raw, 'pencil', split_axis=0, concat_axis=0, tiled=...]
    pallas_call x1, Pallas kernels: 27.4 us -> 18.5 us  [planes_call(): pl.pallas_call(kernel, grid=(1,), in_specs=in_specs, out_specs=[pl.BlockS...]
    ppermute x3, waiting for transfers between devices: 7.79 us -> 0.01 us  [body(): pieces = [lax.ppermute(sent, 'pencil', flipped(bit)) for bit in (4, 8, 12)]]
    all_to_all x0 -> x1, starting transfers between devices: none -> 6.02 us  [body(): lax.all_to_all(partial_raw, 'pencil', split_axis=0, concat_axis=0, tiled=...]
    pallas_call x1, Pallas kernels: 19.8 us -> 13.9 us  [planes_call(): pl.pallas_call(kernel, grid=(1,), in_specs=in_specs, out_specs=pl.BlockSp...]
    ppermute x1, waiting for transfers between devices: 0.01 us -> 3.18 us  [body(): other = lax.ppermute(other, 'pencil', [(i, i ^ 1) for i in range(count)])]
    pallas_call x0 -> x1, Pallas kernels: none -> 1.52 us  [body(): pl.pallas_call(functools.partial(gather_kernel, count), in_specs=[smem(),...]
    unnamed x13 -> x12, local copies, waits for them, and re-layouts: 3.5 us -> 2.75 us
  transfers between devices with their start and end apart: 6 -> 7, of which waited for: 2 -> 1; matrix products, arithmetic and copies ran while one was open for 6% -> 9% of each run, Pallas kernels for 24% -> 24%
where the time goes in v1:
time: 98.1 us; the launch traced here: 97.5 us
  Pallas kernels  62.4 us (64%)
  starting transfers between devices  19.8 us (20%)
  other arithmetic  7.89 us (8%)
  local copies, waits for them, and re-layouts  3.34 us (3%)
  waiting for transfers between devices  3.19 us (3%)
    pallas_call x1, Pallas kernels, planes_call(): pl.pallas_call(kernel, grid=(1,), in_specs=in_specs, out_specs=[pl.BlockS...  18.5 us
    pallas_call x1, Pallas kernels, planes_call(): pl.pallas_call(kernel, grid=(1,), in_specs=in_specs, out_specs=pl.BlockSp...  13.9 us
    pallas_call x1, Pallas kernels, body(): pl.pallas_call(functools.partial(charge_kernel, count), grid=(chunks,), i...  11.7 us
    pallas_call x1, Pallas kernels, body(): pl.pallas_call(functools.partial(boundary_kernel, count), grid=(chunks,),...  9.38 us
    pallas_call x1, Pallas kernels, body(): pl.pallas_call(functools.partial(last_kernel, count), in_specs=[smem(), v...  7.44 us
    all_to_all x1, starting transfers between devices, body(): lax.all_to_all(copies, 'pencil', split_axis=0, concat_axis=0, tiled=True)  7.39 us
    sort x1, other arithmetic, body(): lax.sort((key.reshape(local_g), lax.iota(I32, local_g)), num_keys=1, is_s...  7.05 us
    all_to_all x1, starting transfers between devices, body(): lax.all_to_all(partial_raw, 'pencil', split_axis=0, concat_axis=0, tiled=...  6.02 us
  transfers between devices with their start and end apart: 7, of which 1 were waited for; matrix products, arithmetic and copies ran while one was open for 9% of the time, Pallas kernels for 24%

profile of v1, /device:TPU:0, one launch (start us, length us, event | category | flops | bytes accessed | tf_op | source)
XLA Modules:
  0.0 97.5 jit_solution(7881568025929000796)
XLA Ops:
  0.6 1.5 %atoms.1 = (f32[16,4,128]{2,1,0:T(4,128)}, s32[64,128]{1,0:T(8,128)}) custom-call(s32[1]{0:T(128)} %bitcast.place_ref.refs_0_, f32[4,81]{1,0:T(4,128)} %bitcast.34, f32[3,4]{1,0:T(4,128)} %positions_ref.1, s32[1,4]{1,0:T(1,128)} %bitcast.35, s32[64,128]{1,0:T(8,128)} %bitcast.27), custom_call_target="tpu_custom_call" | custom-call | tf_op jit(solution)/shard_map/atoms/pallas_call | solution.py:695
  2.2 7.4 %all-to-all-start = ((f32[16,4,128]{2,1,0:T(4,128)}), f32[16,4,128]{2,1,0:T(4,128)S(1)}, u32[]{:S(2)}, u32[]{:S(2)}) async-start(f32[16,4,128]{2,1,0:T(4,128)} %get-tuple-element.13), calls=%async_computation | async-start | bytes 65536 | tf_op jit(solution)/shard_map/all_to_all | solution.py:713
  9.6 7.1 %sort.15 = (s32[8192]{0:T(1024)}, s32[8192]{0:T(1024)}) sort(s32[8192]{0:T(1024)} %bitcast.33, s32[8192]{0:T(1024)S(1)} %iota.3), dimensions={0}, to_apply=%region_0.0 | sort | flops 106496 | bytes 131072 | tf_op jit(solution)/shard_map/sort | solution.py:716
  16.6 0.0 all-to-all-done
  16.6 0.0 copy-start.3
  16.6 0.6 copy-done.3
  17.2 11.7 %charge.1 = (f32[2,8192]{1,0:T(2,128)}, f32[200,128]{1,0:T(8,128)}) custom-call(s32[1]{0:T(128)} %bitcast.place_ref.refs_0_, f32[64,128]{1,0:T(8,128)} %bitcast.30, f32[3,128,256]{2,1,0:T(8,128)} %constant.19.clone.spread_ref, f32[8,128]{1,0:T(8,128)} %constant.18.clone.coef_ref, f32[9,3,8192]{2,1,0:T(4,128)} %bitcast.36, f32[2,8192]{1,0:T(2,128)} %inter_ref.1, ...), custom_call_target="tpu_custom_call" | custom-call | flops 10000000000 | tf_op jit(solution)/shard_map/charge/pallas_call | solution.py:728
  28.9 1.9 %collective-permute-start = (f32[200,128]{1,0:T(8,128)}, f32[200,128]{1,0:T(8,128)S(1)}, u32[]{:S(2)}, u32[]{:S(2)}) collective-permute-start(f32[200,128]{1,0:T(8,128)} %get-tuple-element.17), channel_id=1, source_target_pairs={{0,4},{1,5},{2,6},{3,7},{4,0},{5,1},{6,2},{7,3},{8,12},{9,13},{10,... | collective-permute-start | bytes 307208 | tf_op jit(solution)/shard_map/ppermute | solution.py:789
  30.8 2.4 %collective-permute-start.1 = (f32[200,128]{1,0:T(8,128)}, f32[200,128]{1,0:T(8,128)S(1)}, u32[]{:S(2)}, u32[]{:S(2)}) collective-permute-start(f32[200,128]{1,0:T(8,128)} %get-tuple-element.17), channel_id=1, source_target_pairs={{0,8},{1,9},{2,10},{3,11},{4,12},{5,13},{6,14},{7,15},{8,0},{9,1},... | collective-permute-start | bytes 307208 | tf_op jit(solution)/shard_map/ppermute | solution.py:789
  33.2 0.1 collective-permute-start.2
  33.3 0.0 copy-start.2
  33.3 9.4 %boundary.1 = f32[64,128]{1,0:T(8,128)} custom-call(s32[1]{0:T(128)} %bitcast.place_ref.refs_0_, f32[64,128]{1,0:T(8,128)} %bitcast.31, f32[6,256,128]{2,1,0:T(8,128)} %constant.20.clone.gather_ref, f32[8,128]{1,0:T(8,128)} %constant.18.clone.coef_ref, s32[1,64]{1,0:T(1,128)} %bitcast.40, f32[9,3,8192]{2,1,0:T(4,128)} %bitcast.37, ...), custom_call_target="tpu_custom_call" | custom-call | flops 10000000000 | tf_op jit(solution)/shard_map/boundary/pallas_call | solution.py:759
  42.7 6.0 %all-to-all-start.1 = ((f32[16,4,128]{2,1,0:T(4,128)}), f32[16,4,128]{2,1,0:T(4,128)S(1)}, u32[]{:S(2)}, u32[]{:S(2)}) async-start(f32[16,4,128]{2,1,0:T(4,128)} %bitcast.32), calls=%async_computation.1 | async-start | bytes 65536 | tf_op jit(solution)/shard_map/all_to_all | solution.py:782
  48.7 0.0 collective-permute-done
  48.7 0.0 collective-permute-done.1
  48.7 0.0 collective-permute-done.2
  48.7 0.0 copy-done.2
  48.8 0.0 copy-start
  48.8 2.0 %collective-permute-start.3 = (f32[4,200,128]{2,1,0:T(8,128)S(1)}, f32[4,200,128]{2,1,0:T(8,128)S(1)}, u32[]{:S(2)}, u32[]{:S(2)}) collective-permute-start(f32[4,200,128]{2,1,0:T(8,128)S(1)} %pad_maximum_fusion.refs_1_.refs_2_), channel_id=1, source_target_pairs={{0,2},{1,3},{2,0},{3,1},{4,6},{5,7},{6,4},{7,5},{8,10},{9,11},{10,... | collective-permute-start | bytes 1228808 | tf_op jit(solution)/shard_map/ppermute | solution.py:792
  50.8 0.0 copy-done
  50.8 13.9 %planes_near.1.refs_5_ = f32[65,64,256]{2,1,0:T(8,128)} custom-call(s32[1]{0:T(128)} %bitcast.place_ref.refs_0_, f32[4,200,128]{2,1,0:T(8,128)} %copy-done, f32[4,200,128]{2,1,0:T(8,128)} %copy-done, bf16[256,128]{1,0:T(8,128)(2,1)} %constant.21.clone.refs_3_), custom_call_target="tpu_custom_call" | custom-call | flops 15000000512 | tf_op jit(solution)/shard_map/planes_near/pallas_call | solution.py:579
  64.7 0.0 all-to-all-done.1
  64.7 0.0 copy-start.1
  64.7 0.0 collective-permute-done.3.refs_1_.refs_2_
  64.7 0.0 copy-start.5
  64.7 0.6 copy-done.1
  65.3 0.2 copy-done.5
  65.4 18.5 %planes.1 = (f32[2,2176,128]{2,1,0:T(8,128)}, f32[2,2176,128]{2,1,0:T(8,128)}) custom-call(s32[1]{0:T(128)} %bitcast.place_ref.refs_0_, f32[4,200,128]{2,1,0:T(8,128)} %copy-done.5, f32[4,200,128]{2,1,0:T(8,128)} %copy-done.5, bf16[256,128]{1,0:T(8,128)(2,1)} %constant.21.clone.refs_3_, f32[256,512]{1,0:T(8,128)} %constant.22.clone.refs_4_, ...), custom_call_target="tpu_custom_call" | custom-call | flops 24999999488 | tf_op jit(solution)/shard_map/planes/pallas_call | solution.py:607
  83.9 0.1 collective-permute-start.4
  84.0 0.8 reduce_sum.9
  84.8 0.6 slice_bitcast_fusion
  85.4 3.2 %collective-permute-done.4.other_ref = f32[2,2176,128]{2,1,0:T(8,128)S(1)} collective-permute-done((f32[2,2176,128]{2,1,0:T(8,128)}, f32[2,2176,128]{2,1,0:T(8,128)S(1)}, u32[]{:S(2)}, u32[]{:S(2)}) %collective-permute-start.4) | collective-permute-done | bytes 2228256 | tf_op jit(solution)/shard_map/ppermute | solution.py:803
  88.6 0.0 copy-start.4
  88.6 1.4 %copy-done.4 = f32[2,2176,128]{2,1,0:T(8,128)} copy-done((f32[2,2176,128]{2,1,0:T(8,128)}, f32[2,2176,128]{2,1,0:T(8,128)S(1)}, u32[]{:S(2)}) %copy-start.4) | copy-done | bytes 2228248
  89.9 7.4 %last.1 = f32[4096,256]{1,0:T(8,128)} custom-call(s32[1]{0:T(128)} %bitcast.place_ref.refs_0_, f32[2,2176,128]{2,1,0:T(8,128)} %get-tuple-element.22.own_ref, f32[2,2176,128]{2,1,0:T(8,128)} %copy-done.4, f32[2,256,256]{2,1,0:T(8,128)} %constant.23.clone.wave_ref, f32[64,128]{1,0:T(8,128)} %bitcast.22), custom_call_target="tpu_custom_call" | custom-call | flops 7000000000 | tf_op jit(solution)/shard_map/last/pallas_call | solution.py:807
  (2 shorter events, 0.1 us)
Async XLA Ops:
  2.2 14.5 %all-to-all-start = ((f32[16,4,128]{2,1,0:T(4,128)}), f32[16,4,128]{2,1,0:T(4,128)S(1)}, u32[]{:S(2)}, u32[]{:S(2)}) async-start(f32[16,4,128]{2,1,0:T(4,128)} %get-tuple-element.13), calls=%async_computation | async-start | bytes 65536 | tf_op jit(solution)/shard_map/all_to_all | solution.py:713
  16.6 0.6 copy-start.3
  28.9 19.8 %collective-permute-start = (f32[200,128]{1,0:T(8,128)}, f32[200,128]{1,0:T(8,128)S(1)}, u32[]{:S(2)}, u32[]{:S(2)}) collective-permute-start(f32[200,128]{1,0:T(8,128)} %get-tuple-element.17), channel_id=1, source_target_pairs={{0,4},{1,5},{2,6},{3,7},{4,0},{5,1},{6,2},{7,3},{8,12},{9,13},{10,... | collective-permute-start | bytes 307208 | tf_op jit(solution)/shard_map/ppermute | solution.py:789
  30.8 17.9 %collective-permute-start.1 = (f32[200,128]{1,0:T(8,128)}, f32[200,128]{1,0:T(8,128)S(1)}, u32[]{:S(2)}, u32[]{:S(2)}) collective-permute-start(f32[200,128]{1,0:T(8,128)} %get-tuple-element.17), channel_id=1, source_target_pairs={{0,8},{1,9},{2,10},{3,11},{4,12},{5,13},{6,14},{7,15},{8,0},{9,1},... | collective-permute-start | bytes 307208 | tf_op jit(solution)/shard_map/ppermute | solution.py:789
  33.2 15.5 %collective-permute-start.2 = (f32[200,128]{1,0:T(8,128)}, f32[200,128]{1,0:T(8,128)S(1)}, u32[]{:S(2)}, u32[]{:S(2)}) collective-permute-start(f32[200,128]{1,0:T(8,128)} %get-tuple-element.17), channel_id=1, source_target_pairs={{0,12},{1,13},{2,14},{3,15},{4,8},{5,9},{6,10},{7,11},{8,4},{9,5},... | collective-permute-start | bytes 307208 | tf_op jit(solution)/shard_map/ppermute | solution.py:789
  33.3 15.4 %copy-start.2 = (f32[200,128]{1,0:T(8,128)S(1)}, f32[200,128]{1,0:T(8,128)}, u32[]{:S(2)}) copy-start(f32[200,128]{1,0:T(8,128)} %get-tuple-element.17) | copy-start | bytes 307204
  42.7 22.0 %all-to-all-start.1 = ((f32[16,4,128]{2,1,0:T(4,128)}), f32[16,4,128]{2,1,0:T(4,128)S(1)}, u32[]{:S(2)}, u32[]{:S(2)}) async-start(f32[16,4,128]{2,1,0:T(4,128)} %bitcast.32), calls=%async_computation.1 | async-start | bytes 65536 | tf_op jit(solution)/shard_map/all_to_all | solution.py:782
  48.8 2.0 %copy-start = (f32[4,200,128]{2,1,0:T(8,128)}, f32[4,200,128]{2,1,0:T(8,128)S(1)}, u32[]{:S(2)}) copy-start(f32[4,200,128]{2,1,0:T(8,128)S(1)} %pad_maximum_fusion.refs_1_.refs_2_) | copy-start | bytes 1228804
  48.8 15.9 %collective-permute-start.3 = (f32[4,200,128]{2,1,0:T(8,128)S(1)}, f32[4,200,128]{2,1,0:T(8,128)S(1)}, u32[]{:S(2)}, u32[]{:S(2)}) collective-permute-start(f32[4,200,128]{2,1,0:T(8,128)S(1)} %pad_maximum_fusion.refs_1_.refs_2_), channel_id=1, source_target_pairs={{0,2},{1,3},{2,0},{3,1},{4,6},{5,7},{6,4},{7,5},{8,10},{9,11},{10,... | collective-permute-start | bytes 1228808 | tf_op jit(solution)/shard_map/ppermute | solution.py:792
  64.7 0.6 copy-start.1
  64.7 0.8 copy-start.5
  83.9 4.6 %collective-permute-start.4 = (f32[2,2176,128]{2,1,0:T(8,128)}, f32[2,2176,128]{2,1,0:T(8,128)S(1)}, u32[]{:S(2)}, u32[]{:S(2)}) collective-permute-start(f32[2,2176,128]{2,1,0:T(8,128)} %get-tuple-element.23), channel_id=1, source_target_pairs={{0,1},{1,0},{2,3},{3,2},{4,5},{5,4},{6,7},{7,6},{8,9},{9,8},{10,11... | collective-permute-start | bytes 6684680 | tf_op jit(solution)/shard_map/ppermute | solution.py:803
  88.6 1.4 %copy-start.4 = (f32[2,2176,128]{2,1,0:T(8,128)}, f32[2,2176,128]{2,1,0:T(8,128)S(1)}, u32[]{:S(2)}) copy-start(f32[2,2176,128]{2,1,0:T(8,128)S(1)} %collective-permute-done.4.other_ref) | copy-start | bytes 6684676

commit v2 on v1

--- a/solution.py
+++ b/solution.py
@@ -15,13 +15,13 @@
 KINDS = 3
 ROWS = 256
 CHUNK = 2048
-PITCH = NG // 2 + 8
 HIGH = lax.Precision.HIGHEST
 TWO_PI = 2.0 * math.pi
 F32 = jnp.float32
 BF16 = jnp.bfloat16
 I32 = jnp.int32
-VMEM_BYTES = 56 * 1024 * 1024
+PLANES_MB = 58
+LAST_MB = 58
 
 
 def norm(degree, m_order):
@@ -245,6 +245,8 @@
     order_ref,
     pot_ref,
     sent_ref,
+    cos_ref,
+    sin_ref,
     weights,
     rows_scratch,
     values,
@@ -272,6 +274,8 @@
     rest = jnp.dot(weights[0:atoms, :], table_low, preferred_element_type=F32)
     shape_part = main[0:atoms] + (main[atoms:] + rest)
     cosine, sine = angles(atoms_ref, freq)
+    cos_ref[...] = cosine
+    sin_ref[...] = sine
     pseudo_re = jnp.sum(shape_part * cosine, axis=0, keepdims=True)
     pseudo_im = -jnp.sum(shape_part * sine, axis=0, keepdims=True)
     freq_x, freq_y, freq_z = freq
@@ -299,8 +303,8 @@
             here = line_of == r
             row_re = jnp.broadcast_to(values[0, pl.ds(r, 1), :], (lines, 128))
             row_im = jnp.broadcast_to(values[1, pl.ds(r, 1), :], (lines, 128))
-            taken_re = jnp.where(here, jnp.take_along_axis(row_re, lane, axis=1), taken_re)
-            taken_im = jnp.where(here, jnp.take_along_axis(row_im, lane, axis=1), taken_im)
+            taken_re = jnp.where(here, jnp.take_along_axis(row_re, lane, 1, mode="promise_in_bounds"), taken_re)
+            taken_im = jnp.where(here, jnp.take_along_axis(row_im, lane, 1, mode="promise_in_bounds"), taken_im)
             return taken_re, taken_im
 
         empty = jnp.zeros((lines, 128), F32)
@@ -331,6 +335,8 @@
     bessel_ref,
     pot_ref,
     index_ref,
+    cos_ref,
+    sin_ref,
     out_ref,
     total,
     rows_scratch,
@@ -339,7 +345,7 @@
     atoms = atoms_ref.shape[0]
     _, *freq = frequencies(index_ref[...], place_ref[0], count)
     table_high, table_low = table_of(freq, bessel_ref, coef_ref, rows_scratch)
-    cosine, sine = angles(atoms_ref, freq)
+    cosine, sine = cos_ref[...], sin_ref[...]
     pot_re, pot_im = pot_ref[0:1, :], pot_ref[1:2, :]
     real_part = pot_re * cosine - pot_im * sine
     imag_part = pot_re * sine + pot_im * cosine
@@ -375,26 +381,30 @@
         out_ref[...] = jnp.dot(moved, raw, precision=HIGH, preferred_element_type=F32)
 
 
-def planes_kernel(count, pattern, finish, *refs):
-    if finish:
-        place_ref, start_ref, recv_ref, step_ref, wave_ref, before_ref, _ = refs[:7]
-        own_ref, other_ref, box, front, back, fields, wave, earlier, sem = refs[7:]
-    else:
-        place_ref, start_ref, recv_ref, step_ref, box, front, back, fields = refs
+def plane_type(place):
+    return ((place >> 1) ^ ((place & 1) * (place >> 2))) & 1
+
+
+def planes_kernel(count, pattern, *refs):
+    place_ref, recv_ref, step_ref, wave_in, _, own_out, other_out = refs[:7]
+    wave_ref, own_ref, other_ref, wave, start_ref, sem, box, front, back, fields = refs[7:]
     rows = NG // count
     chip_rows = 2 * rows
     sources = recv_ref.shape[0]
     lines = (recv_ref.shape[1] - 8) // 3
-    half_planes = NG // 4
+    halves = 1 if pattern is None else 2
+    local_planes = NG // 4 // halves
+    pitch = 2 * local_planes + 8
     tiles = lines // 2
     together = math.gcd(tiles, 16)
     place = place_ref[0]
     core = place % 2
     base = (place // 2) * chip_rows
 
-    if finish and before_ref is not None:
-        fetch = pltpu.make_async_copy(before_ref, earlier, sem)
-        fetch.start()
+    fetch = pltpu.make_async_copy(recv_ref.at[:, pl.ds(3 * lines, 8), :], start_ref, sem.at[0])
+    fetch.start()
+    fetch_wave = pltpu.make_async_copy(wave_in, wave_ref, sem.at[1])
+    fetch_wave.start()
     box[...] = jnp.zeros_like(box)
 
     sub = lax.broadcasted_iota(I32, (8, 128), 0)
@@ -438,9 +448,12 @@
         return start_ref[s, which, t].astype(I32)
 
     def plane_at(s, k):
-        owner = place ^ (4 * s + pattern) if pattern is not None else 2 * s + core
+        if pattern is None:
+            owner = 2 * s + core
+        else:
+            owner = place ^ pattern ^ (8 * (s >> 1) + (4 + 2 * core) * (s & 1))
         jx = k * count + owner
-        return jnp.where(jx > NG // 2, NG - jx, jx) // 2
+        return jnp.where(jx > NG // 2, NG - jx, jx) // (2 * halves)
 
     def add_tile(s, t, wanted, held):
         left, right = [], []
@@ -481,8 +494,9 @@
                 first, last = edge(s, t, 0), edge(s, t, 1)
                 second = jnp.where(last > first, 1.0, 0.0)
                 add_tile(s, t, [(first, 1.0), (last, second)], held)
-                one_chunk(following, 2 * t, filled)
-                one_chunk(following, 2 * t + 1, filled)
+                if filled is not None:
+                    one_chunk(following, 2 * t, filled)
+                    one_chunk(following, 2 * t + 1, filled)
                 most = jnp.maximum(most, last - first)
             return most
 
@@ -505,28 +519,25 @@
         return 0
 
     lax.fori_loop(0, lines // 8, first_chunks, 0)
+    fetch.wait()
 
     def two_sources(t, _):
         one_source(2 * t, front, 2 * t + 1, back)
-        one_source(2 * t + 1, back, jnp.minimum(2 * t + 2, sources - 1), front)
+        one_source(2 * t + 1, back, 2 * t + 2, front)
         return 0
 
-    lax.fori_loop(0, sources // 2, two_sources, 0)
-    if not finish:
-        return
-
+    lax.fori_loop(0, sources // 2 - 1, two_sources, 0)
+    one_source(sources - 2, front, sources - 1, back)
+    one_source(sources - 1, back, None, None)
+    fetch_wave.wait()
     cos_z, sin_z = wave_ref[:, :NG], wave_ref[:, NG:]
     for j, table in enumerate((wave_ref[...], jnp.concatenate([-sin_z, cos_z], 1))):
         high, low = split(table)
         for k, part in enumerate((high, high, low)):
             wave[(3 * j + k) * NG : (3 * j + k + 1) * NG, :] = part
-    if before_ref is not None:
-        fetch.wait()
 
     def along_z(at, number):
         block = box[pl.ds(at, number)]
-        if before_ref is not None:
-            block = block + earlier[pl.ds(at, number)]
         left = []
         for part in (block[:, :chip_rows], block[:, chip_rows:]):
             high, low = split(part.reshape(number * chip_rows, NG))
@@ -536,7 +547,7 @@
         return out[:, :, :NG], out[:, :, NG:]
 
     def keep(at, value):
-        line = pl.ds(at, rows, stride=PITCH)
+        line = pl.ds(at, rows, stride=pitch)
         for h in range(2):
             own_ref[h, line, :] = value[:rows, h * 128 : (h + 1) * 128]
             other_ref[h, line, :] = value[rows:, h * 128 : (h + 1) * 128]
@@ -550,81 +561,94 @@
             keep(2 * (g * group + j) + 1, im[j])
         return 0
 
-    lax.fori_loop(0, half_planes // group, some_planes, 0, unroll=2)
-
-    @pl.when(core == 0)
+    lax.fori_loop(0, local_planes // group, some_planes, 0, unroll=2)
+    has_middle = core == 0
+    if pattern is not None:
+        has_middle = has_middle & (plane_type(place) == (1 if pattern else 0))
+
+    @pl.when(has_middle)
     def _():
-        re, _ = along_z(half_planes, 1)
+        re, _ = along_z(local_planes, 1)
         keep(1, re[0])
 
-
-def planes_call(count, place, recv, pattern, steps, finish=False, wave=None, before=None, after=None):
+    stores = [
+        pltpu.make_async_copy(other_ref, other_out, sem.at[0]),
+        pltpu.make_async_copy(own_ref, own_out, sem.at[1]),
+    ]
+    for store in stores:
+        store.start()
+    for store in stores:
+        store.wait()
+
+
+def planes_call(count, place, recv, pattern, steps, wave, after):
     rows = NG // count
     sources = recv.shape[0]
     lines = (recv.shape[1] - 8) // 3
-    half_rows = rows * PITCH
-    box = (NG // 4 + 1, 4 * rows, NG)
+    local_planes = NG // 4 // (1 if pattern is None else 2)
+    half = jax.ShapeDtypeStruct((2, rows * (2 * local_planes + 8), 128), F32)
     vmem = pl.BlockSpec(memory_space=pltpu.VMEM)
+    anywhere = pl.BlockSpec(memory_space=pl.ANY)
     held = pltpu.VMEM((lines, 8 * rows, 128), BF16)
-    scratch = [held, held, pltpu.VMEM((sources, 7, lines, 128), F32)]
-    start_spec = pl.BlockSpec(
-        (sources, 8, 128), lambda i: (0, 3 * lines // 8, 0), memory_space=pltpu.SMEM
-    )
-    recv_spec = pl.BlockSpec(recv.shape, lambda i: (0, 0, 0))
-    step_spec = pl.BlockSpec(steps.shape, lambda i: (0, 0))
-    in_specs = [smem(), start_spec, recv_spec, step_spec]
-    operands = [place, recv, recv, steps]
-    kernel = functools.partial(planes_kernel, count, pattern, finish)
-    if not finish:
-        return pl.pallas_call(
-            kernel,
-            grid=(1,),
-            in_specs=in_specs,
-            out_specs=pl.BlockSpec(box, lambda i: (0, 0, 0)),
-            out_shape=jax.ShapeDtypeStruct(box, F32),
-            scratch_shapes=scratch,
-            compiler_params=params(),
-            name="planes_near",
+    return pl.pallas_call(
+        functools.partial(planes_kernel, count, pattern),
+        in_specs=[smem(), vmem, vmem, anywhere, anywhere],
+        out_specs=[anywhere, anywhere],
+        out_shape=[half, half],
+        scratch_shapes=[
+            pltpu.VMEM((NG, 2 * NG), F32),
+            pltpu.VMEM(half.shape, F32),
+            pltpu.VMEM(half.shape, F32),
+            pltpu.VMEM((6 * NG, 2 * NG), BF16),
+            pltpu.SMEM((sources, 8, 128), F32),
+            pltpu.SemaphoreType.DMA((2,)),
+            pltpu.VMEM((local_planes + 1, 4 * rows, NG), F32),
+            held,
+            held,
+            pltpu.VMEM((sources, 7, lines, 128), F32),
+        ],
+        compiler_params=params(PLANES_MB),
+        name="planes_far" if pattern else "planes_near",
         cost_estimate=cost(15),
-        )(*operands)
-    scratch = [pltpu.VMEM(box, F32)] + scratch + [pltpu.VMEM((6 * NG, 2 * NG), BF16)]
-    anywhere = pl.BlockSpec(memory_space=pl.ANY)
-    in_specs.append(pl.BlockSpec(wave.shape, lambda i: (0, 0)))
-    operands.append(wave)
-    if before is None:
-        inner = kernel
-        at = len(in_specs)
-
-        def kernel(*refs):
-            inner(*refs[:at], None, *refs[at:], None, None)
-
-    else:
-        in_specs.append(anywhere)
-        operands.append(before)
-        scratch += [pltpu.VMEM(box, F32), pltpu.SemaphoreType.DMA]
-    in_specs.append(anywhere)
-    operands.append(after)
-    return pl.pallas_call(
-        kernel,
-        grid=(1,),
-        in_specs=in_specs,
-        out_specs=[pl.BlockSpec((2, half_rows, 128), lambda i: (0, 0, 0))] * 2,
-        out_shape=[jax.ShapeDtypeStruct((2, half_rows, 128), F32)] * 2,
-        scratch_shapes=scratch,
-        compiler_params=params(),
-        name="planes",
-        cost_estimate=cost(25),
-    )(*operands)
-
-
-def last_kernel(count, place_ref, own_ref, other_ref, wave_ref, _, out_ref, held, wave, sem):
+    )(place, recv, steps, wave, after)
+
+
+def last_kernel(count, place_ref, wave_ref, *refs):
+    halves = (len(refs) - 6) // 2
+    given = refs[: 2 * halves]
+    out_ref, held, wave, tables_ref, parts, sem = refs[2 * halves :]
     rows = NG // count
-    wave[0], wave[1] = split(wave_ref[place_ref[0] % 2])
-
-    def one_row(y, _):
-        line = pl.ds(pl.multiple_of(y * PITCH, 8), NG // 2)
+    size = NG // 2 // halves
+    pitch = size + 8
+    place = place_ref[0]
+    group = 4
+    fetch_tables = pltpu.make_async_copy(wave_ref, tables_ref, sem.at[0, 2 * halves])
+    fetch_tables.start()
+    fetches = []
+    for g in range(rows // group):
+        line = pl.ds(g * group * pitch, group * pitch)
+        fetches.append(
+            [
+                pltpu.make_async_copy(part.at[:, line, :], parts.at[i, :, line, :], sem.at[g, i])
+                for i, part in enumerate(given)
+            ]
+        )
+        for fetch in fetches[-1]:
+            fetch.start()
+    fetch_tables.wait()
+    tables = []
+    for device in (place, place ^ 1):
+        for half in range(halves):
+            which = device & 1
+            if halves == 2:
+                which = 2 * which + (plane_type(device) ^ half)
+            tables.append(tables_ref[which])
+    wave[0], wave[1] = split(jnp.concatenate(tables, 0).T)
+
+    def one_row(y):
+        line = pl.ds(y * pitch, size)
         mixed = [
-            jnp.concatenate([own_ref[h, line, :], other_ref[h, line, :]], 0) for h in range(2)
+            jnp.concatenate([parts[i, h, line, :] for i in range(2 * halves)], 0) for h in range(2)
         ]
         high, low = split(jnp.concatenate(mixed, 1))
         main = jnp.dot(wave[...].reshape(2 * NG, NG), high, preferred_element_type=F32)
@@ -632,11 +656,14 @@
         out = main[:NG] + (main[NG:] + rest)
         for h in range(2):
             held[h, pl.ds(y, NG, stride=rows), :] = out[:, h * 128 : (h + 1) * 128]
-        return 0
-
-    lax.fori_loop(0, rows, one_row, 0, unroll=4)
+
+    for g in range(rows // group):
+        for fetch in fetches[g]:
+            fetch.wait()
+        for y in range(g * group, (g + 1) * group):
+            one_row(y)
     copies = [
-        pltpu.make_async_copy(held.at[h], out_ref.at[:, pl.ds(h * 128, 128)], sem.at[h])
+        pltpu.make_async_copy(held.at[h], out_ref.at[:, pl.ds(h * 128, 128)], sem.at[0, h])
         for h in range(2)
     ]
     for copy in copies:
@@ -645,21 +672,23 @@
         copy.wait()
 
 
-def wave_tables():
+def wave_tables(halves):
     j = np.arange(NG)
     phase = 2 * np.pi / NG * ((j[:, None] * j[None, :]) % NG)
     along_z = np.concatenate([np.cos(phase), np.sin(phase)], 1)
-    classes = []
+    along_x = []
     for core in range(2):
-        table = np.zeros((NG, NG // 2))
-        for i in range(NG // 4):
-            phase_x = 2 * np.pi / NG * ((j * (2 * i + core)) % NG)
-            table[:, 2 * i] = np.cos(phase_x)
-            table[:, 2 * i + 1] = -np.sin(phase_x)
-        if core == 0:
-            table[:, 1] = np.cos(np.pi * j)
-        classes.append(table)
-    along_x = [np.concatenate([classes[c], classes[1 - c]], 1) for c in range(2)]
+        for kind in range(halves):
+            planes = np.arange(core, NG // 2, 2)
+            if halves == 2 and core == 0:
+                planes = planes[planes % 4 == 2 * kind]
+            elif halves == 2:
+                planes = planes[np.isin(planes % 8, (3, 5) if kind else (1, 7))]
+            phase = 2 * np.pi / NG * ((planes[:, None] * j[None, :]) % NG)
+            table = np.stack([np.cos(phase), -np.sin(phase)], 1).reshape(-1, NG)
+            if planes[0] == 0:
+                table[1] = np.cos(np.pi * j)
+            along_x.append(table)
     return along_z.astype(np.float32), np.stack(along_x).astype(np.float32)
 
 
@@ -671,8 +700,8 @@
     return pl.CostEstimate(flops=int(micros * 1e9), bytes_accessed=0, transcendentals=0)
 
 
-def params():
-    return pltpu.CompilerParams(vmem_limit_bytes=VMEM_BYTES)
+def params(megabytes=56):
+    return pltpu.CompilerParams(vmem_limit_bytes=megabytes * 1024 * 1024)
 
 
 def body(
@@ -689,7 +718,7 @@
     rows = NG // count
     spread, gather = placement_tables()
     coef = jnp.asarray(recurrence_table())
-    along_z, along_x = wave_tables()
+    along_z, along_x = wave_tables(2 if count == 16 else 1)
 
     vmem = pl.BlockSpec(memory_space=pltpu.VMEM)
     copies, key = pl.pallas_call(
@@ -725,7 +754,8 @@
     pair_spec = pl.BlockSpec((2, CHUNK), lambda i: (0, i))
     radial_spec = pl.BlockSpec((LMAX + 1, KINDS, CHUNK), lambda i: (0, 0, i))
     spread = jnp.asarray(spread)
-    pot, sent = pl.pallas_call(
+    atom_spec = pl.BlockSpec((atoms, CHUNK), lambda i: (0, i))
+    pot, sent, cosine, sine = pl.pallas_call(
         functools.partial(charge_kernel, count),
         grid=(chunks,),
         in_specs=[
@@ -739,10 +769,17 @@
             whole(key),
             whole(order),
         ],
-        out_specs=[pair_spec, pl.BlockSpec((3 * lines + 8, 128), lambda i: (0, 0))],
+        out_specs=[
+            pair_spec,
+            pl.BlockSpec((3 * lines + 8, 128), lambda i: (0, 0)),
+            atom_spec,
+            atom_spec,
+        ],
         out_shape=[
             jax.ShapeDtypeStruct((2, local_g), F32),
             jax.ShapeDtypeStruct((3 * lines + 8, 128), F32),
+            jax.ShapeDtypeStruct((atoms, local_g), F32),
+            jax.ShapeDtypeStruct((atoms, local_g), F32),
         ],
         scratch_shapes=[
             pltpu.VMEM((2 * atoms, ROWS), BF16),
@@ -768,6 +805,8 @@
             radial_spec,
             pair_spec,
             line_spec,
+            atom_spec,
+            atom_spec,
         ],
         out_specs=pl.BlockSpec((atoms, 128), lambda i: (0, 0)),
         out_shape=jax.ShapeDtypeStruct((atoms, 128), F32),
@@ -778,46 +817,51 @@
         compiler_params=params(),
         name="boundary",
         cost_estimate=cost(10),
-    )(place, atom_rows, gather, coef, slot_line, boundary_bessel.transpose(1, 0, 2), pot, index_line)
+    )(place, atom_rows, gather, coef, slot_line, boundary_bessel.transpose(1, 0, 2), pot, index_line, cosine, sine)
     parts = lax.all_to_all(partial_raw, "pencil", split_axis=0, concat_axis=0, tiled=True)
     boundary = jnp.sum(parts.reshape(count, own_atoms, 128), axis=0)[:, :LM].T
 
     steps = jnp.asarray(np.broadcast_to(np.arange(NG)[:, None], (NG, 128)).astype(BF16))
     along_z = jnp.asarray(along_z)
+    sibling = [(i, i ^ 1) for i in range(count)]
     if count == 16:
-        flipped = lambda bit: [(i, i ^ bit) for i in range(count)]
-        pieces = [lax.ppermute(sent, "pencil", flipped(bit)) for bit in (4, 8, 12)]
+        masks = [lambda i: 4 + 2 * (i & 1), lambda i: 8, lambda i: 12 + 2 * (i & 1)]
+        pieces = [
+            lax.ppermute(sent, "pencil", [(i, i ^ mask(i)) for i in range(count)])
+            for mask in masks
+        ]
         pieces, partial_raw = lax.optimization_barrier((pieces, partial_raw))
         near = jnp.stack([sent] + pieces)
-        far = lax.ppermute(near, "pencil", flipped(2))
-        begun = planes_call(count, place, near, 0, steps)
-        own, other = planes_call(
-            count, place, far, 2, steps, True, along_z, begun, parts
-        )
+        far = lax.ppermute(near, "pencil", [(i, i ^ 2) for i in range(count)])
+        own_near, other_near = planes_call(count, place, near, 0, steps, along_z, partial_raw)
+        other_near = lax.ppermute(other_near, "pencil", sibling)
+        own_far, other_far = planes_call(count, place, far, 2, steps, along_z, parts)
+        other_far = lax.ppermute(other_far, "pencil", sibling)
+        waves = [own_near, own_far, other_near, other_far]
     else:
         groups = [list(range(c, count, 2)) for c in range(2)]
         recv = lax.all_gather(sent, "pencil", axis_index_groups=groups)
-        own, other = planes_call(
-            count, place, recv, None, steps, True, along_z, None, partial_raw
-        )
-    other = lax.ppermute(other, "pencil", [(i, i ^ 1) for i in range(count)])
-
-    vmem = pl.BlockSpec(memory_space=pltpu.VMEM)
+        own, other = planes_call(count, place, recv, None, steps, along_z, partial_raw)
+        waves = [own, lax.ppermute(other, "pencil", sibling)]
+
+    along_x = jnp.asarray(along_x)
     anywhere = pl.BlockSpec(memory_space=pl.ANY)
     potential = pl.pallas_call(
         functools.partial(last_kernel, count),
-        in_specs=[smem(), vmem, vmem, vmem, anywhere],
+        in_specs=[smem()] + [anywhere] * (1 + len(waves)),
         out_specs=anywhere,
         out_shape=jax.ShapeDtypeStruct((NG * rows, NG), F32),
         scratch_shapes=[
             pltpu.VMEM((2, NG * rows, 128), F32),
             pltpu.VMEM((2, NG, NG), BF16),
-            pltpu.SemaphoreType.DMA((2,)),
+            pltpu.VMEM(along_x.shape, F32),
+            pltpu.VMEM((len(waves),) + waves[0].shape, F32),
+            pltpu.SemaphoreType.DMA((rows // 4, len(waves) + 1)),
         ],
-        compiler_params=params(),
+        compiler_params=params(LAST_MB),
         name="last",
         cost_estimate=cost(7),
-    )(place, own, other, jnp.asarray(along_x), parts)
+    )(place, along_x, *waves)
     return (potential.reshape(NG, rows, NG), boundary)
 
 

time: 98.1 us -> 92.3 us (0.941)
  Pallas kernels: 62.4 us -> 58.2 us
  waiting for transfers between devices: 3.19 us -> 1.33 us
    pallas_call x3, Pallas kernels: 39.8 us -> 36.9 us  [the longest x2 30.3 us: planes_call(): pl.pallas_call(functools.partial(planes_kernel, count, pattern), in_specs...]
    ppermute x5 -> x6, waiting for transfers between devices: 3.19 us -> 1.33 us  [the longest x1 1.31 us: body(): other_far = lax.ppermute(other_far, 'pencil', sibling)]
    pallas_call x1, Pallas kernels: 9.38 us -> 7.64 us  [body(): pl.pallas_call(functools.partial(boundary_kernel, count), grid=(chunks,),...]
    ppermute x5 -> x6, starting transfers between devices: 6.44 us -> 7.01 us  [the longest x3 4.39 us: body(): lax.ppermute(sent, 'pencil', [(i, i ^ mask(i)) for i in range(count)])]
    unnamed x12 -> x14, local copies, waits for them, and re-layouts: 2.75 us -> 2.39 us
  transfers between devices with their start and end apart: 7 -> 8, of which waited for: 1 -> 1; matrix products, arithmetic and copies ran while one was open for 9% -> 9% of each run, Pallas kernels for 24% -> 41%
where the time goes in v2:
time: 92.3 us; the launch traced here: 91.7 us
  Pallas kernels  58.2 us (63%)
  starting transfers between devices  20.4 us (22%)
  other arithmetic  7.87 us (9%)
  local copies, waits for them, and re-layouts  2.97 us (3%)
  waiting for transfers between devices  1.33 us (1%)
  between operations  0.95 us (1%)
    pallas_call x2, Pallas kernels, planes_call(): pl.pallas_call(functools.partial(planes_kernel, count, pattern), in_specs...  30.3 us
    pallas_call x1, Pallas kernels, body(): pl.pallas_call(functools.partial(charge_kernel, count), grid=(chunks,), i...  12.1 us
    pallas_call x1, Pallas kernels, body(): pl.pallas_call(functools.partial(boundary_kernel, count), grid=(chunks,),...  7.64 us
    all_to_all x1, starting transfers between devices, body(): lax.all_to_all(copies, 'pencil', split_axis=0, concat_axis=0, tiled=True)  7.39 us
    sort x1, other arithmetic, body(): lax.sort((key.reshape(local_g), lax.iota(I32, local_g)), num_keys=1, is_s...  7.05 us
    pallas_call x1, Pallas kernels, body(): pl.pallas_call(functools.partial(last_kernel, count), in_specs=[smem()] +...  6.66 us
    all_to_all x1, starting transfers between devices, body(): lax.all_to_all(partial_raw, 'pencil', split_axis=0, concat_axis=0, tiled=...  6 us
    ppermute x3, starting transfers between devices, body(): lax.ppermute(sent, 'pencil', [(i, i ^ mask(i)) for i in range(count)])  4.39 us
  transfers between devices with their start and end apart: 8, of which 1 were waited for; matrix products, arithmetic and copies ran while one was open for 9% of the time, Pallas kernels for 41%

profile of v2, /device:TPU:0, one launch (start us, length us, event | category | flops | bytes accessed | tf_op | source)
XLA Modules:
  0.0 91.7 jit_solution(7314057842050142717)
XLA Ops:
  0.6 1.5 %atoms.1 = (f32[16,4,128]{2,1,0:T(4,128)}, s32[64,128]{1,0:T(8,128)}) custom-call(s32[1]{0:T(128)} %bitcast.place_ref.refs_0_, f32[4,81]{1,0:T(4,128)} %bitcast.33, f32[3,4]{1,0:T(4,128)} %positions_ref.1, s32[1,4]{1,0:T(1,128)} %bitcast.34, s32[64,128]{1,0:T(8,128)} %bitcast.26), custom_call_target="tpu_custom_call" | custom-call | tf_op jit(solution)/shard_map/atoms/pallas_call | solution.py:724
  2.2 7.4 %all-to-all-start = ((f32[16,4,128]{2,1,0:T(4,128)}), f32[16,4,128]{2,1,0:T(4,128)S(1)}, u32[]{:S(2)}, u32[]{:S(2)}) async-start(f32[16,4,128]{2,1,0:T(4,128)} %get-tuple-element.18), calls=%async_computation | async-start | bytes 65536 | tf_op jit(solution)/shard_map/all_to_all | solution.py:742
  9.6 7.0 %sort.15 = (s32[8192]{0:T(1024)}, s32[8192]{0:T(1024)}) sort(s32[8192]{0:T(1024)} %bitcast.32, s32[8192]{0:T(1024)S(1)} %iota.3), dimensions={0}, to_apply=%region_0.0 | sort | flops 106496 | bytes 131072 | tf_op jit(solution)/shard_map/sort | solution.py:745
  16.6 0.0 all-to-all-done
  16.6 0.0 copy-start.3
  16.6 0.6 copy-done.3
  17.2 12.1 %charge.1 = (f32[2,8192]{1,0:T(2,128)}, f32[200,128]{1,0:T(8,128)}, f32[64,8192]{1,0:T(8,128)}, f32[64,8192]{1,0:T(8,128)}) custom-call(s32[1]{0:T(128)} %bitcast.place_ref.refs_0_, f32[64,128]{1,0:T(8,128)} %bitcast.29, f32[3,128,256]{2,1,0:T(8,128)} %constant.19.clone.spread_ref, f32[8,128]{1,0:T(8,128)} %constant.18.clone.coef_ref, ...), custom_call_target="tpu_custom_call" | custom-call | flops 10000000000 | tf_op jit(solution)/shard_map/charge/pallas_call | solution.py:758
  29.3 3.7 %collective-permute-start.2 = (f32[200,128]{1,0:T(8,128)}, f32[200,128]{1,0:T(8,128)S(1)}, u32[]{:S(2)}, u32[]{:S(2)}) collective-permute-start(f32[200,128]{1,0:T(8,128)} %get-tuple-element.22), channel_id=1, source_target_pairs={{0,12},{1,15},{2,14},{3,13},{4,8},{5,11},{6,10},{7,9},{8,4},{9,7},... | collective-permute-start | bytes 307208 | tf_op jit(solution)/shard_map/ppermute | solution.py:830
  33.0 0.0 collective-permute-start.1
  33.0 0.7 collective-permute-start
  33.7 0.0 copy-start.2
  33.7 7.6 %boundary.1.refs_4_ = f32[64,128]{1,0:T(8,128)} custom-call(s32[1]{0:T(128)} %bitcast.place_ref.refs_0_, f32[64,128]{1,0:T(8,128)} %bitcast.30, f32[6,256,128]{2,1,0:T(8,128)} %constant.20.clone.gather_ref, f32[8,128]{1,0:T(8,128)} %constant.18.clone.coef_ref, s32[1,64]{1,0:T(1,128)} %bitcast.39, f32[9,3,8192]{2,1,0:T(4,128)} %bitcast.36, ...), custom_call_target="tpu_custom_call" | custom-call | flops 10000000000 | tf_op jit(solution)/shard_map/boundary/pallas_call | solution.py:796
  41.4 6.0 %all-to-all-start.1 = ((f32[16,4,128]{2,1,0:T(4,128)}), f32[16,4,128]{2,1,0:T(4,128)S(1)}, u32[]{:S(2)}, u32[]{:S(2)}) async-start(f32[16,4,128]{2,1,0:T(4,128)} %bitcast.31), calls=%async_computation.1 | async-start | bytes 65536 | tf_op jit(solution)/shard_map/all_to_all | solution.py:821
  47.4 0.0 collective-permute-done.2
  47.4 0.0 collective-permute-done.1
  47.4 0.0 collective-permute-done
  47.4 0.0 copy-done.2
  47.4 0.0 copy-start
  47.4 2.0 %collective-permute-start.3 = (f32[4,200,128]{2,1,0:T(8,128)S(1)}, f32[4,200,128]{2,1,0:T(8,128)S(1)}, u32[]{:S(2)}, u32[]{:S(2)}) collective-permute-start(f32[4,200,128]{2,1,0:T(8,128)S(1)} %pad_maximum_fusion.refs_1_), channel_id=1, source_target_pairs={{0,2},{1,3},{2,0},{3,1},{4,6},{5,7},{6,4},{7,5},{8,10},{9,11},{10,... | collective-permute-start | bytes 1228808 | tf_op jit(solution)/shard_map/ppermute | solution.py:835
  49.4 0.0 copy-done
  49.4 15.2 %planes_near.1 = (f32[2,1152,128]{2,1,0:T(8,128)}, f32[2,1152,128]{2,1,0:T(8,128)}) custom-call(s32[1]{0:T(128)} %bitcast.place_ref.refs_0_, f32[4,200,128]{2,1,0:T(8,128)} %copy-done, bf16[256,128]{1,0:T(8,128)(2,1)} %constant.21.clone.refs_2_, f32[256,512]{1,0:T(8,128)} %constant.22.clone.refs_3_, f32[64,128]{1,0:T(8,128)} %boundary.1.refs_4_), custom_call_target="tpu_custom_call" | custom-call | flops 15000000512 | tf_op jit(solution)/shard_map/planes_near/pallas_call | solution.py:593
  64.6 0.1 collective-permute-start.4
  64.7 0.0 all-to-all-done.1
  64.7 0.0 copy-start.1
  64.7 0.0 collective-permute-done.3.refs_1_
  64.8 0.0 copy-start.6
  64.8 0.6 copy-done.1
  65.3 0.2 copy-done.6
  65.5 15.1 %planes_far.1 = (f32[2,1152,128]{2,1,0:T(8,128)}, f32[2,1152,128]{2,1,0:T(8,128)}) custom-call(s32[1]{0:T(128)} %bitcast.place_ref.refs_0_, f32[4,200,128]{2,1,0:T(8,128)} %copy-done.6, bf16[256,128]{1,0:T(8,128)(2,1)} %constant.21.clone.refs_2_, f32[256,512]{1,0:T(8,128)} %constant.22.clone.refs_3_, f32[64,128]{1,0:T(8,128)} %bitcast.21), custom_call_target="tpu_custom_call" | custom-call | flops 15000000512 | tf_op jit(solution)/shard_map/planes_far/pallas_call | solution.py:593
  80.6 0.6 collective-permute-start.5
  81.1 0.8 reduce_sum.9
  81.9 0.6 slice_bitcast_fusion
  82.5 0.0 collective-permute-done.4.refs_2_
  82.5 0.0 copy-start.4
  82.5 1.3 %collective-permute-done.5.refs_3_ = f32[2,1152,128]{2,1,0:T(8,128)S(1)} collective-permute-done((f32[2,1152,128]{2,1,0:T(8,128)}, f32[2,1152,128]{2,1,0:T(8,128)S(1)}, u32[]{:S(2)}, u32[]{:S(2)}) %collective-permute-start.5) | collective-permute-done | bytes 1179680 | tf_op jit(solution)/shard_map/ppermute | solution.py:839
  83.8 0.0 copy-start.5
  83.8 0.0 copy-done.4
  83.8 1.0 %copy-done.5 = f32[2,1152,128]{2,1,0:T(8,128)} copy-done((f32[2,1152,128]{2,1,0:T(8,128)}, f32[2,1152,128]{2,1,0:T(8,128)S(1)}, u32[]{:S(2)}) %copy-start.5) | copy-done | bytes 1179672
  84.9 6.7 %last.1 = f32[4096,256]{1,0:T(8,128)} custom-call(s32[1]{0:T(128)} %bitcast.place_ref.refs_0_, f32[4,64,256]{2,1,0:T(8,128)} %constant.23.clone.wave_ref, f32[2,1152,128]{2,1,0:T(8,128)} %get-tuple-element.30.refs_0_, f32[2,1152,128]{2,1,0:T(8,128)} %get-tuple-element.31.refs_1_, f32[2,1152,128]{2,1,0:T(8,128)} %copy-done.4, f32[2,1152,128]{2,1,0:T(8,128)} %copy-done.5), custom_call_target="tpu_custom_call" | custom-call | flops 7000000000 | tf_op jit(solution)/shard_map/last/pallas_call | solution.py:849
  (2 shorter events, 0.0 us)
Async XLA Ops:
  2.2 14.5 %all-to-all-start = ((f32[16,4,128]{2,1,0:T(4,128)}), f32[16,4,128]{2,1,0:T(4,128)S(1)}, u32[]{:S(2)}, u32[]{:S(2)}) async-start(f32[16,4,128]{2,1,0:T(4,128)} %get-tuple-element.18), calls=%async_computation | async-start | bytes 65536 | tf_op jit(solution)/shard_map/all_to_all | solution.py:742
  16.6 0.6 copy-start.3
  29.3 18.0 %collective-permute-start.2 = (f32[200,128]{1,0:T(8,128)}, f32[200,128]{1,0:T(8,128)S(1)}, u32[]{:S(2)}, u32[]{:S(2)}) collective-permute-start(f32[200,128]{1,0:T(8,128)} %get-tuple-element.22), channel_id=1, source_target_pairs={{0,12},{1,15},{2,14},{3,13},{4,8},{5,11},{6,10},{7,9},{8,4},{9,7},... | collective-permute-start | bytes 307208 | tf_op jit(solution)/shard_map/ppermute | solution.py:830
  33.0 14.3 %collective-permute-start.1 = (f32[200,128]{1,0:T(8,128)}, f32[200,128]{1,0:T(8,128)S(1)}, u32[]{:S(2)}, u32[]{:S(2)}) collective-permute-start(f32[200,128]{1,0:T(8,128)} %get-tuple-element.22), channel_id=1, source_target_pairs={{0,8},{1,9},{2,10},{3,11},{4,12},{5,13},{6,14},{7,15},{8,0},{9,1},... | collective-permute-start | bytes 307208 | tf_op jit(solution)/shard_map/ppermute | solution.py:830
  33.0 14.3 %collective-permute-start = (f32[200,128]{1,0:T(8,128)}, f32[200,128]{1,0:T(8,128)S(1)}, u32[]{:S(2)}, u32[]{:S(2)}) collective-permute-start(f32[200,128]{1,0:T(8,128)} %get-tuple-element.22), channel_id=1, source_target_pairs={{0,4},{1,7},{2,6},{3,5},{4,0},{5,3},{6,2},{7,1},{8,12},{9,15},{10,... | collective-permute-start | bytes 307208 | tf_op jit(solution)/shard_map/ppermute | solution.py:830
  33.7 13.7 %copy-start.2 = (f32[200,128]{1,0:T(8,128)S(1)}, f32[200,128]{1,0:T(8,128)}, u32[]{:S(2)}) copy-start(f32[200,128]{1,0:T(8,128)} %get-tuple-element.22) | copy-start | bytes 307204
  41.4 23.4 %all-to-all-start.1 = ((f32[16,4,128]{2,1,0:T(4,128)}), f32[16,4,128]{2,1,0:T(4,128)S(1)}, u32[]{:S(2)}, u32[]{:S(2)}) async-start(f32[16,4,128]{2,1,0:T(4,128)} %bitcast.31), calls=%async_computation.1 | async-start | bytes 65536 | tf_op jit(solution)/shard_map/all_to_all | solution.py:821
  47.4 2.0 %copy-start = (f32[4,200,128]{2,1,0:T(8,128)}, f32[4,200,128]{2,1,0:T(8,128)S(1)}, u32[]{:S(2)}) copy-start(f32[4,200,128]{2,1,0:T(8,128)S(1)} %pad_maximum_fusion.refs_1_) | copy-start | bytes 1228804
  47.4 17.3 %collective-permute-start.3 = (f32[4,200,128]{2,1,0:T(8,128)S(1)}, f32[4,200,128]{2,1,0:T(8,128)S(1)}, u32[]{:S(2)}, u32[]{:S(2)}) collective-permute-start(f32[4,200,128]{2,1,0:T(8,128)S(1)} %pad_maximum_fusion.refs_1_), channel_id=1, source_target_pairs={{0,2},{1,3},{2,0},{3,1},{4,6},{5,7},{6,4},{7,5},{8,10},{9,11},{10,... | collective-permute-start | bytes 1228808 | tf_op jit(solution)/shard_map/ppermute | solution.py:835
  64.6 17.9 %collective-permute-start.4 = (f32[2,1152,128]{2,1,0:T(8,128)}, f32[2,1152,128]{2,1,0:T(8,128)S(1)}, u32[]{:S(2)}, u32[]{:S(2)}) collective-permute-start(f32[2,1152,128]{2,1,0:T(8,128)} %get-tuple-element.32), channel_id=1, source_target_pairs={{0,1},{1,0},{2,3},{3,2},{4,5},{5,4},{6,7},{7,6},{8,9},{9,8},{10,11... | collective-permute-start | bytes 3538952 | tf_op jit(solution)/shard_map/ppermute | solution.py:837
  64.7 0.6 copy-start.1
  64.8 0.7 copy-start.6
  80.6 3.2 %collective-permute-start.5 = (f32[2,1152,128]{2,1,0:T(8,128)}, f32[2,1152,128]{2,1,0:T(8,128)S(1)}, u32[]{:S(2)}, u32[]{:S(2)}) collective-permute-start(f32[2,1152,128]{2,1,0:T(8,128)} %get-tuple-element.33), channel_id=1, source_target_pairs={{0,1},{1,0},{2,3},{3,2},{4,5},{5,4},{6,7},{7,6},{8,9},{9,8},{10,11... | collective-permute-start | bytes 3538952 | tf_op jit(solution)/shard_map/ppermute | solution.py:839
  82.5 1.3 %copy-start.4 = (f32[2,1152,128]{2,1,0:T(8,128)}, f32[2,1152,128]{2,1,0:T(8,128)S(1)}, u32[]{:S(2)}) copy-start(f32[2,1152,128]{2,1,0:T(8,128)S(1)} %collective-permute-done.4.refs_2_) | copy-start | bytes 3538948
  83.8 1.0 %copy-start.5 = (f32[2,1152,128]{2,1,0:T(8,128)}, f32[2,1152,128]{2,1,0:T(8,128)S(1)}, u32[]{:S(2)}) copy-start(f32[2,1152,128]{2,1,0:T(8,128)S(1)} %collective-permute-done.5.refs_3_) | copy-start | bytes 3538948

commit v3 on v2

--- a/solution.py
+++ b/solution.py
@@ -15,12 +15,13 @@
 KINDS = 3
 ROWS = 256
 CHUNK = 2048
+GROUP = 16
 HIGH = lax.Precision.HIGHEST
 TWO_PI = 2.0 * math.pi
 F32 = jnp.float32
 BF16 = jnp.bfloat16
 I32 = jnp.int32
-PLANES_MB = 58
+PLANES_MB = 20
 LAST_MB = 58
 
 
@@ -386,15 +387,16 @@
 
 
 def planes_kernel(count, pattern, *refs):
-    place_ref, recv_ref, step_ref, wave_in, _, own_out, other_out = refs[:7]
-    wave_ref, own_ref, other_ref, wave, start_ref, sem, box, front, back, fields = refs[7:]
+    place_ref, recv_ref, step_ref, own_out, other_out = refs[:5]
+    own_ref, other_ref, wave, start_ref, sem, store_sem = refs[5:11]
+    box, front, back, fields = refs[11:]
     rows = NG // count
     chip_rows = 2 * rows
     sources = recv_ref.shape[0]
     lines = (recv_ref.shape[1] - 8) // 3
     halves = 1 if pattern is None else 2
     local_planes = NG // 4 // halves
-    pitch = 2 * local_planes + 8
+    pitch = 2 * GROUP + 8
     tiles = lines // 2
     together = math.gcd(tiles, 16)
     place = place_ref[0]
@@ -403,8 +405,6 @@
 
     fetch = pltpu.make_async_copy(recv_ref.at[:, pl.ds(3 * lines, 8), :], start_ref, sem.at[0])
     fetch.start()
-    fetch_wave = pltpu.make_async_copy(wave_in, wave_ref, sem.at[1])
-    fetch_wave.start()
     box[...] = jnp.zeros_like(box)
 
     sub = lax.broadcasted_iota(I32, (8, 128), 0)
@@ -529,10 +529,10 @@
     lax.fori_loop(0, sources // 2 - 1, two_sources, 0)
     one_source(sources - 2, front, sources - 1, back)
     one_source(sources - 1, back, None, None)
-    fetch_wave.wait()
-    cos_z, sin_z = wave_ref[:, :NG], wave_ref[:, NG:]
-    for j, table in enumerate((wave_ref[...], jnp.concatenate([-sin_z, cos_z], 1))):
-        high, low = split(table)
+    grid = [lax.broadcasted_iota(I32, (NG, NG), d).astype(F32) for d in range(2)]
+    cos_z, sin_z = turn(grid[0] * grid[1] * (1.0 / NG))
+    for j, table in enumerate(([cos_z, sin_z], [-sin_z, cos_z])):
+        high, low = split(jnp.concatenate(table, 1))
         for k, part in enumerate((high, high, low)):
             wave[(3 * j + k) * NG : (3 * j + k + 1) * NG, :] = part
 
@@ -546,62 +546,57 @@
         out = out.reshape(number, chip_rows, 2 * NG)
         return out[:, :, :NG], out[:, :, NG:]
 
-    def keep(at, value):
+    def keep(g, at, value):
         line = pl.ds(at, rows, stride=pitch)
         for h in range(2):
-            own_ref[h, line, :] = value[:rows, h * 128 : (h + 1) * 128]
-            other_ref[h, line, :] = value[rows:, h * 128 : (h + 1) * 128]
-
-    group = 16
-
-    def some_planes(g, _):
-        re, im = along_z(g * group, group)
-        for j in range(group):
-            keep(2 * (g * group + j), re[j])
-            keep(2 * (g * group + j) + 1, im[j])
-        return 0
-
-    lax.fori_loop(0, local_planes // group, some_planes, 0, unroll=2)
+            own_ref[g, h, line, :] = value[:rows, h * 128 : (h + 1) * 128]
+            other_ref[g, h, line, :] = value[rows:, h * 128 : (h + 1) * 128]
+
     has_middle = core == 0
     if pattern is not None:
         has_middle = has_middle & (plane_type(place) == (1 if pattern else 0))
-
-    @pl.when(has_middle)
-    def _():
-        re, _ = along_z(local_planes, 1)
-        keep(1, re[0])
-
-    stores = [
-        pltpu.make_async_copy(other_ref, other_out, sem.at[0]),
-        pltpu.make_async_copy(own_ref, own_out, sem.at[1]),
-    ]
-    for store in stores:
-        store.start()
+    stores = []
+    for g in range(local_planes // GROUP):
+        re, im = along_z(g * GROUP, GROUP)
+        for j in range(GROUP):
+            keep(g, 2 * j, re[j])
+            keep(g, 2 * j + 1, im[j])
+        if g == 0:
+
+            @pl.when(has_middle)
+            def _():
+                re, _ = along_z(local_planes, 1)
+                keep(0, 1, re[0])
+
+        for j, (made, out) in enumerate(((other_ref, other_out), (own_ref, own_out))):
+            stores.append(pltpu.make_async_copy(made.at[g], out.at[g], store_sem.at[g, j]))
+            stores[-1].start()
     for store in stores:
         store.wait()
 
 
-def planes_call(count, place, recv, pattern, steps, wave, after):
+def planes_call(count, place, recv, pattern, steps):
     rows = NG // count
     sources = recv.shape[0]
     lines = (recv.shape[1] - 8) // 3
     local_planes = NG // 4 // (1 if pattern is None else 2)
-    half = jax.ShapeDtypeStruct((2, rows * (2 * local_planes + 8), 128), F32)
+    groups = local_planes // GROUP
+    half = jax.ShapeDtypeStruct((groups, 2, rows * (2 * GROUP + 8), 128), F32)
     vmem = pl.BlockSpec(memory_space=pltpu.VMEM)
-    anywhere = pl.BlockSpec(memory_space=pl.ANY)
+    anywhere = pl.BlockSpec(memory_space=pltpu.HBM)
     held = pltpu.VMEM((lines, 8 * rows, 128), BF16)
     return pl.pallas_call(
         functools.partial(planes_kernel, count, pattern),
-        in_specs=[smem(), vmem, vmem, anywhere, anywhere],
+        in_specs=[smem(), vmem, vmem],
         out_specs=[anywhere, anywhere],
         out_shape=[half, half],
         scratch_shapes=[
-            pltpu.VMEM((NG, 2 * NG), F32),
             pltpu.VMEM(half.shape, F32),
             pltpu.VMEM(half.shape, F32),
             pltpu.VMEM((6 * NG, 2 * NG), BF16),
             pltpu.SMEM((sources, 8, 128), F32),
             pltpu.SemaphoreType.DMA((2,)),
+            pltpu.SemaphoreType.DMA((groups, 2)),
             pltpu.VMEM((local_planes + 1, 4 * rows, NG), F32),
             held,
             held,
@@ -610,7 +605,7 @@
         compiler_params=params(PLANES_MB),
         name="planes_far" if pattern else "planes_near",
         cost_estimate=cost(15),
-    )(place, recv, steps, wave, after)
+    )(place, recv, steps)
 
 
 def last_kernel(count, place_ref, wave_ref, *refs):
@@ -618,8 +613,7 @@
     given = refs[: 2 * halves]
     out_ref, held, wave, tables_ref, parts, sem = refs[2 * halves :]
     rows = NG // count
-    size = NG // 2 // halves
-    pitch = size + 8
+    pitch = 2 * GROUP + 8
     place = place_ref[0]
     group = 4
     fetch_tables = pltpu.make_async_copy(wave_ref, tables_ref, sem.at[0, 2 * halves])
@@ -629,7 +623,9 @@
         line = pl.ds(g * group * pitch, group * pitch)
         fetches.append(
             [
-                pltpu.make_async_copy(part.at[:, line, :], parts.at[i, :, line, :], sem.at[g, i])
+                pltpu.make_async_copy(
+                    part.at[:, :, line, :], parts.at[i, :, :, line, :], sem.at[g, i]
+                )
                 for i, part in enumerate(given)
             ]
         )
@@ -646,9 +642,13 @@
     wave[0], wave[1] = split(jnp.concatenate(tables, 0).T)
 
     def one_row(y):
-        line = pl.ds(y * pitch, size)
+        line = pl.ds(y * pitch, 2 * GROUP)
         mixed = [
-            jnp.concatenate([parts[i, h, line, :] for i in range(2 * halves)], 0) for h in range(2)
+            jnp.concatenate(
+                [parts[i, q, h, line, :] for i in range(2 * halves) for q in range(parts.shape[1])],
+                0,
+            )
+            for h in range(2)
         ]
         high, low = split(jnp.concatenate(mixed, 1))
         main = jnp.dot(wave[...].reshape(2 * NG, NG), high, preferred_element_type=F32)
@@ -674,8 +674,6 @@
 
 def wave_tables(halves):
     j = np.arange(NG)
-    phase = 2 * np.pi / NG * ((j[:, None] * j[None, :]) % NG)
-    along_z = np.concatenate([np.cos(phase), np.sin(phase)], 1)
     along_x = []
     for core in range(2):
         for kind in range(halves):
@@ -689,7 +687,7 @@
             if planes[0] == 0:
                 table[1] = np.cos(np.pi * j)
             along_x.append(table)
-    return along_z.astype(np.float32), np.stack(along_x).astype(np.float32)
+    return np.stack(along_x).astype(np.float32)
 
 
 def smem():
@@ -718,7 +716,7 @@
     rows = NG // count
     spread, gather = placement_tables()
     coef = jnp.asarray(recurrence_table())
-    along_z, along_x = wave_tables(2 if count == 16 else 1)
+    along_x = wave_tables(2 if count == 16 else 1)
 
     vmem = pl.BlockSpec(memory_space=pltpu.VMEM)
     copies, key = pl.pallas_call(
@@ -819,10 +817,8 @@
         cost_estimate=cost(10),
     )(place, atom_rows, gather, coef, slot_line, boundary_bessel.transpose(1, 0, 2), pot, index_line, cosine, sine)
     parts = lax.all_to_all(partial_raw, "pencil", split_axis=0, concat_axis=0, tiled=True)
-    boundary = jnp.sum(parts.reshape(count, own_atoms, 128), axis=0)[:, :LM].T
 
     steps = jnp.asarray(np.broadcast_to(np.arange(NG)[:, None], (NG, 128)).astype(BF16))
-    along_z = jnp.asarray(along_z)
     sibling = [(i, i ^ 1) for i in range(count)]
     if count == 16:
         masks = [lambda i: 4 + 2 * (i & 1), lambda i: 8, lambda i: 12 + 2 * (i & 1)]
@@ -833,19 +829,21 @@
         pieces, partial_raw = lax.optimization_barrier((pieces, partial_raw))
         near = jnp.stack([sent] + pieces)
         far = lax.ppermute(near, "pencil", [(i, i ^ 2) for i in range(count)])
-        own_near, other_near = planes_call(count, place, near, 0, steps, along_z, partial_raw)
+        own_near, other_near = planes_call(count, place, near, 0, steps)
         other_near = lax.ppermute(other_near, "pencil", sibling)
-        own_far, other_far = planes_call(count, place, far, 2, steps, along_z, parts)
+        far, parts = lax.optimization_barrier((far, parts))
+        own_far, other_far = planes_call(count, place, far, 2, steps)
         other_far = lax.ppermute(other_far, "pencil", sibling)
         waves = [own_near, own_far, other_near, other_far]
     else:
         groups = [list(range(c, count, 2)) for c in range(2)]
         recv = lax.all_gather(sent, "pencil", axis_index_groups=groups)
-        own, other = planes_call(count, place, recv, None, steps, along_z, partial_raw)
+        own, other = planes_call(count, place, recv, None, steps)
         waves = [own, lax.ppermute(other, "pencil", sibling)]
 
+    boundary = jnp.sum(parts.reshape(count, own_atoms, 128), axis=0)[:, :LM].T
     along_x = jnp.asarray(along_x)
-    anywhere = pl.BlockSpec(memory_space=pl.ANY)
+    anywhere = pl.BlockSpec(memory_space=pltpu.HBM)
     potential = pl.pallas_call(
         functools.partial(last_kernel, count),
         in_specs=[smem()] + [anywhere] * (1 + len(waves)),
@@ -856,7 +854,7 @@
             pltpu.VMEM((2, NG, NG), BF16),
             pltpu.VMEM(along_x.shape, F32),
             pltpu.VMEM((len(waves),) + waves[0].shape, F32),
-            pltpu.SemaphoreType.DMA((rows // 4, len(waves) + 1)),
+            pltpu.SemaphoreType.DMA((rows // 4, 5)),
         ],
         compiler_params=params(LAST_MB),
         name="last",

time: 92.3 us -> 89.8 us (0.973)
  Pallas kernels: 58.2 us -> 55.5 us
    pallas_call x2, Pallas kernels: 30.3 us -> 27.5 us  [planes_call(): pl.pallas_call(functools.partial(planes_kernel, count, pattern), in_specs...]
    unnamed x14 -> x10, local copies, waits for them, and re-layouts: 2.39 us -> 2.73 us
  transfers between devices with their start and end apart: 8 -> 8, of which waited for: 1 -> 1; matrix products, arithmetic and copies ran while one was open for 9% -> 9% of each run, Pallas kernels for 41% -> 39%
where the time goes in v3:
time: 89.8 us; the launch traced here: 89.3 us
  Pallas kernels  55.5 us (62%)
  starting transfers between devices  20.3 us (23%)
  other arithmetic  7.11 us (8%)
  local copies, waits for them, and re-layouts  3.32 us (4%)
  waiting for transfers between devices  2.2 us (2%)
  between operations  0.92 us (1%)
    pallas_call x2, Pallas kernels, planes_call(): pl.pallas_call(functools.partial(planes_kernel, count, pattern), in_specs...  27.5 us
    pallas_call x1, Pallas kernels, body(): pl.pallas_call(functools.partial(charge_kernel, count), grid=(chunks,), i...  12 us
    pallas_call x1, Pallas kernels, body(): pl.pallas_call(functools.partial(boundary_kernel, count), grid=(chunks,),...  7.69 us
    all_to_all x1, starting transfers between devices, body(): lax.all_to_all(copies, 'pencil', split_axis=0, concat_axis=0, tiled=True)  7.39 us
    sort x1, other arithmetic, body(): lax.sort((key.reshape(local_g), lax.iota(I32, local_g)), num_keys=1, is_s...  7.05 us
    pallas_call x1, Pallas kernels, body(): pl.pallas_call(functools.partial(last_kernel, count), in_specs=[smem()] +...  6.7 us
    all_to_all x1, starting transfers between devices, body(): lax.all_to_all(partial_raw, 'pencil', split_axis=0, concat_axis=0, tiled=...  6.01 us
    ppermute x3, starting transfers between devices, body(): lax.ppermute(sent, 'pencil', [(i, i ^ mask(i)) for i in range(count)])  4.45 us
  transfers between devices with their start and end apart: 8, of which 1 were waited for; matrix products, arithmetic and copies ran while one was open for 9% of the time, Pallas kernels for 39%

profile of v3, /device:TPU:0, one launch (start us, length us, event | category | flops | bytes accessed | tf_op | source)
XLA Modules:
  0.0 89.3 jit_solution(3499546109376746519)
XLA Ops:
  0.6 1.5 %atoms.1 = (f32[16,4,128]{2,1,0:T(4,128)}, s32[64,128]{1,0:T(8,128)}) custom-call(s32[1]{0:T(128)} %bitcast.place_ref.refs_0_, f32[4,81]{1,0:T(4,128)} %bitcast.33, f32[3,4]{1,0:T(4,128)} %positions_ref.1, s32[1,4]{1,0:T(1,128)} %bitcast.34, s32[64,128]{1,0:T(8,128)} %bitcast.26), custom_call_target="tpu_custom_call" | custom-call | tf_op jit(solution)/shard_map/atoms/pallas_call | solution.py:722
  2.2 7.4 %all-to-all-start = ((f32[16,4,128]{2,1,0:T(4,128)}), f32[16,4,128]{2,1,0:T(4,128)S(1)}, u32[]{:S(2)}, u32[]{:S(2)}) async-start(f32[16,4,128]{2,1,0:T(4,128)} %get-tuple-element.19), calls=%async_computation | async-start | bytes 65536 | tf_op jit(solution)/shard_map/all_to_all | solution.py:740
  9.6 7.0 %sort.15 = (s32[8192]{0:T(1024)}, s32[8192]{0:T(1024)}) sort(s32[8192]{0:T(1024)} %bitcast.32, s32[8192]{0:T(1024)S(1)} %iota.3), dimensions={0}, to_apply=%region_0.0 | sort | flops 106496 | bytes 131072 | tf_op jit(solution)/shard_map/sort | solution.py:743
  16.6 0.0 all-to-all-done
  16.6 0.0 copy-start.4
  16.6 0.6 copy-done.4
  17.2 12.0 %charge.1 = (f32[2,8192]{1,0:T(2,128)}, f32[200,128]{1,0:T(8,128)}, f32[64,8192]{1,0:T(8,128)}, f32[64,8192]{1,0:T(8,128)}) custom-call(s32[1]{0:T(128)} %bitcast.place_ref.refs_0_, f32[64,128]{1,0:T(8,128)} %bitcast.29, f32[3,128,256]{2,1,0:T(8,128)} %constant.17.clone.spread_ref, f32[8,128]{1,0:T(8,128)} %constant.16.clone.coef_ref, ...), custom_call_target="tpu_custom_call" | custom-call | flops 10000000000 | tf_op jit(solution)/shard_map/charge/pallas_call | solution.py:756
  29.3 3.8 %collective-permute-start.2 = (f32[200,128]{1,0:T(8,128)}, f32[200,128]{1,0:T(8,128)S(1)}, u32[]{:S(2)}, u32[]{:S(2)}) collective-permute-start(f32[200,128]{1,0:T(8,128)} %get-tuple-element.23), channel_id=1, source_target_pairs={{0,12},{1,15},{2,14},{3,13},{4,8},{5,11},{6,10},{7,9},{8,4},{9,7},... | collective-permute-start | bytes 307208 | tf_op jit(solution)/shard_map/ppermute | solution.py:826
  33.0 0.0 collective-permute-start.1
  33.1 0.7 collective-permute-start
  33.7 0.0 copy-start.3
  33.7 0.0 copy-start
  33.7 7.7 %boundary.1 = f32[64,128]{1,0:T(8,128)} custom-call(s32[1]{0:T(128)} %bitcast.place_ref.refs_0_, f32[64,128]{1,0:T(8,128)} %bitcast.30, f32[6,256,128]{2,1,0:T(8,128)} %constant.18.clone.gather_ref, f32[8,128]{1,0:T(8,128)} %constant.16.clone.coef_ref, s32[1,64]{1,0:T(1,128)} %bitcast.39, f32[9,3,8192]{2,1,0:T(4,128)} %bitcast.36, ...), custom_call_target="tpu_custom_call" | custom-call | flops 10000000000 | tf_op jit(solution)/shard_map/boundary/pallas_call | solution.py:794
  41.4 6.0 %all-to-all-start.1 = ((f32[16,4,128]{2,1,0:T(4,128)}), f32[16,4,128]{2,1,0:T(4,128)S(1)}, u32[]{:S(2)}, u32[]{:S(2)}) async-start(f32[16,4,128]{2,1,0:T(4,128)} %bitcast.31), calls=%async_computation.1 | async-start | bytes 65536 | tf_op jit(solution)/shard_map/all_to_all | solution.py:819
  47.4 0.0 collective-permute-done.2
  47.4 0.0 collective-permute-done.1
  47.4 0.0 collective-permute-done
  47.5 0.0 copy-done.3
  47.5 2.0 %collective-permute-start.3 = (f32[4,200,128]{2,1,0:T(8,128)S(1)}, f32[4,200,128]{2,1,0:T(8,128)S(1)}, u32[]{:S(2)}, u32[]{:S(2)}) collective-permute-start(f32[4,200,128]{2,1,0:T(8,128)S(1)} %pad_maximum_fusion.refs_1_), channel_id=1, source_target_pairs={{0,2},{1,3},{2,0},{3,1},{4,6},{5,7},{6,4},{7,5},{8,10},{9,11},{10,... | collective-permute-start | bytes 1228808 | tf_op jit(solution)/shard_map/ppermute | solution.py:831
  49.5 0.0 copy-done
  49.5 13.9 %planes_near.1 = (f32[2,2,640,128]{3,2,1,0:T(8,128)S(1)}, f32[2,2,640,128]{3,2,1,0:T(8,128)S(1)}) custom-call(s32[1]{0:T(128)} %bitcast.place_ref.refs_0_, f32[4,200,128]{2,1,0:T(8,128)S(1)} %pad_maximum_fusion.refs_1_, bf16[256,128]{1,0:T(8,128)(2,1)S(1)} %copy-done), custom_call_target="tpu_custom_call" | custom-call | flops 15000000512 | tf_op jit(solution)/shard_map/planes_near/pallas_call | solution.py:588
  63.3 0.0 copy-start.1
  63.4 1.1 %copy-done.1 = f32[2,2,640,128]{3,2,1,0:T(8,128)} copy-done((f32[2,2,640,128]{3,2,1,0:T(8,128)}, f32[2,2,640,128]{3,2,1,0:T(8,128)S(1)}, u32[]{:S(2)}) %copy-start.1) | copy-done | bytes 1310744
  64.4 0.0 collective-permute-start.4
  64.4 0.0 all-to-all-done.1
  64.4 0.0 collective-permute-done.3.refs_1_
  64.4 13.7 %planes_far.1 = (f32[2,2,640,128]{3,2,1,0:T(8,128)S(1)}, f32[2,2,640,128]{3,2,1,0:T(8,128)S(1)}) custom-call(s32[1]{0:T(128)} %bitcast.place_ref.refs_0_, f32[4,200,128]{2,1,0:T(8,128)S(1)} %collective-permute-done.3.refs_1_, bf16[256,128]{1,0:T(8,128)(2,1)S(1)} %copy-done), custom_call_target="tpu_custom_call" | custom-call | flops 15000000512 | tf_op jit(solution)/shard_map/planes_far/pallas_call | solution.py:588
  78.1 0.0 copy-start.2
  78.1 1.0 %copy-done.2 = f32[2,2,640,128]{3,2,1,0:T(8,128)} copy-done((f32[2,2,640,128]{3,2,1,0:T(8,128)}, f32[2,2,640,128]{3,2,1,0:T(8,128)S(1)}, u32[]{:S(2)}) %copy-start.2) | copy-done | bytes 1310744
  79.2 0.5 collective-permute-start.5
  79.7 0.6 slice_bitcast_fusion
  80.3 0.0 collective-permute-done.4.refs_2_
  80.3 2.2 %collective-permute-done.5.refs_3_ = f32[2,2,640,128]{3,2,1,0:T(8,128)} collective-permute-done((f32[2,2,640,128]{3,2,1,0:T(8,128)S(1)}, f32[2,2,640,128]{3,2,1,0:T(8,128)}, u32[]{:S(2)}, u32[]{:S(2)}) %collective-permute-start.5) | collective-permute-done | bytes 1310752 | tf_op jit(solution)/shard_map/ppermute | solution.py:836
  82.5 6.7 %last.1 = f32[4096,256]{1,0:T(8,128)} custom-call(s32[1]{0:T(128)} %bitcast.place_ref.refs_0_, f32[4,64,256]{2,1,0:T(8,128)} %constant.20.clone.wave_ref, f32[2,2,640,128]{3,2,1,0:T(8,128)} %copy-done.1, f32[2,2,640,128]{3,2,1,0:T(8,128)} %copy-done.2, f32[2,2,640,128]{3,2,1,0:T(8,128)} %collective-permute-done.4.refs_2_, ...), custom_call_target="tpu_custom_call" | custom-call | flops 7000000000 | tf_op jit(solution)/shard_map/last/pallas_call | solution.py:847
  (3 shorter events, 0.1 us)
Async XLA Ops:
  2.2 14.5 %all-to-all-start = ((f32[16,4,128]{2,1,0:T(4,128)}), f32[16,4,128]{2,1,0:T(4,128)S(1)}, u32[]{:S(2)}, u32[]{:S(2)}) async-start(f32[16,4,128]{2,1,0:T(4,128)} %get-tuple-element.19), calls=%async_computation | async-start | bytes 65536 | tf_op jit(solution)/shard_map/all_to_all | solution.py:740
  16.6 0.6 copy-start.4
  29.3 18.2 %collective-permute-start.2 = (f32[200,128]{1,0:T(8,128)}, f32[200,128]{1,0:T(8,128)S(1)}, u32[]{:S(2)}, u32[]{:S(2)}) collective-permute-start(f32[200,128]{1,0:T(8,128)} %get-tuple-element.23), channel_id=1, source_target_pairs={{0,12},{1,15},{2,14},{3,13},{4,8},{5,11},{6,10},{7,9},{8,4},{9,7},... | collective-permute-start | bytes 307208 | tf_op jit(solution)/shard_map/ppermute | solution.py:826
  33.0 14.4 %collective-permute-start.1 = (f32[200,128]{1,0:T(8,128)}, f32[200,128]{1,0:T(8,128)S(1)}, u32[]{:S(2)}, u32[]{:S(2)}) collective-permute-start(f32[200,128]{1,0:T(8,128)} %get-tuple-element.23), channel_id=1, source_target_pairs={{0,8},{1,9},{2,10},{3,11},{4,12},{5,13},{6,14},{7,15},{8,0},{9,1},... | collective-permute-start | bytes 307208 | tf_op jit(solution)/shard_map/ppermute | solution.py:826
  33.1 14.4 %collective-permute-start = (f32[200,128]{1,0:T(8,128)}, f32[200,128]{1,0:T(8,128)S(1)}, u32[]{:S(2)}, u32[]{:S(2)}) collective-permute-start(f32[200,128]{1,0:T(8,128)} %get-tuple-element.23), channel_id=1, source_target_pairs={{0,4},{1,7},{2,6},{3,5},{4,0},{5,3},{6,2},{7,1},{8,12},{9,15},{10,... | collective-permute-start | bytes 307208 | tf_op jit(solution)/shard_map/ppermute | solution.py:826
  33.7 13.7 %copy-start.3 = (f32[200,128]{1,0:T(8,128)S(1)}, f32[200,128]{1,0:T(8,128)}, u32[]{:S(2)}) copy-start(f32[200,128]{1,0:T(8,128)} %get-tuple-element.23) | copy-start | bytes 307204
  33.7 15.8 %copy-start = (bf16[256,128]{1,0:T(8,128)(2,1)S(1)}, bf16[256,128]{1,0:T(8,128)(2,1)}, u32[]{:S(2)}) copy-start(bf16[256,128]{1,0:T(8,128)(2,1)} %constant.19.clone.refs_2_) | copy-start | bytes 196612
  41.4 23.0 %all-to-all-start.1 = ((f32[16,4,128]{2,1,0:T(4,128)}), f32[16,4,128]{2,1,0:T(4,128)S(1)}, u32[]{:S(2)}, u32[]{:S(2)}) async-start(f32[16,4,128]{2,1,0:T(4,128)} %bitcast.31), calls=%async_computation.1 | async-start | bytes 65536 | tf_op jit(solution)/shard_map/all_to_all | solution.py:819
  47.5 16.9 %collective-permute-start.3 = (f32[4,200,128]{2,1,0:T(8,128)S(1)}, f32[4,200,128]{2,1,0:T(8,128)S(1)}, u32[]{:S(2)}, u32[]{:S(2)}) collective-permute-start(f32[4,200,128]{2,1,0:T(8,128)S(1)} %pad_maximum_fusion.refs_1_), channel_id=1, source_target_pairs={{0,2},{1,3},{2,0},{3,1},{4,6},{5,7},{6,4},{7,5},{8,10},{9,11},{10,... | collective-permute-start | bytes 1228808 | tf_op jit(solution)/shard_map/ppermute | solution.py:831
  63.3 1.1 %copy-start.1 = (f32[2,2,640,128]{3,2,1,0:T(8,128)}, f32[2,2,640,128]{3,2,1,0:T(8,128)S(1)}, u32[]{:S(2)}) copy-start(f32[2,2,640,128]{3,2,1,0:T(8,128)S(1)} %get-tuple-element.30.refs_0_) | copy-start | bytes 3932164
  64.4 15.9 %collective-permute-start.4 = (f32[2,2,640,128]{3,2,1,0:T(8,128)S(1)}, f32[2,2,640,128]{3,2,1,0:T(8,128)}, u32[]{:S(2)}, u32[]{:S(2)}) collective-permute-start(f32[2,2,640,128]{3,2,1,0:T(8,128)S(1)} %get-tuple-element.33), channel_id=1, source_target_pairs={{0,1},{1,0},{2,3},{3,2},{4,5},{5,4},{6,7},{7,6},{8,9},{9,8},{10,11... | collective-permute-start | bytes 3932168 | tf_op jit(solution)/shard_map/ppermute | solution.py:833
  78.1 1.1 %copy-start.2 = (f32[2,2,640,128]{3,2,1,0:T(8,128)}, f32[2,2,640,128]{3,2,1,0:T(8,128)S(1)}, u32[]{:S(2)}) copy-start(f32[2,2,640,128]{3,2,1,0:T(8,128)S(1)} %get-tuple-element.32.refs_1_) | copy-start | bytes 3932164
  79.2 3.3 %collective-permute-start.5 = (f32[2,2,640,128]{3,2,1,0:T(8,128)S(1)}, f32[2,2,640,128]{3,2,1,0:T(8,128)}, u32[]{:S(2)}, u32[]{:S(2)}) collective-permute-start(f32[2,2,640,128]{3,2,1,0:T(8,128)S(1)} %get-tuple-element.34), channel_id=1, source_target_pairs={{0,1},{1,0},{2,3},{3,2},{4,5},{5,4},{6,7},{7,6},{8,9},{9,8},{10,11... | collective-permute-start | bytes 3932168 | tf_op jit(solution)/shard_map/ppermute | solution.py:836

commit v4 on v3

--- a/solution.py
+++ b/solution.py
@@ -309,7 +309,7 @@
             return taken_re, taken_im
 
         empty = jnp.zeros((lines, 128), F32)
-        taken_re, taken_im = lax.fori_loop(0, lines, one_line, (empty, empty), unroll=8)
+        taken_re, taken_im = lax.fori_loop(0, lines, one_line, (empty, empty), unroll=32)
         key = key_ref[...]
         sent_ref[0:lines, :] = taken_re
         sent_ref[lines : 2 * lines, :] = taken_im

time: 89.8 us -> 89.4 us (level)
  transfers between devices with their start and end apart: 8 -> 8, of which waited for: 1 -> 1; matrix products, arithmetic and copies ran while one was open for 9% -> 9% of each run, Pallas kernels for 39% -> 40%
where the time goes in v4:
time: 89.4 us; the launch traced here: 89 us
  Pallas kernels  55.1 us (62%)
  starting transfers between devices  20.3 us (23%)
  other arithmetic  7.11 us (8%)
  local copies, waits for them, and re-layouts  3.32 us (4%)
  waiting for transfers between devices  2.2 us (2%)
  between operations  0.92 us (1%)
    pallas_call x2, Pallas kernels, planes_call(): pl.pallas_call(functools.partial(planes_kernel, count, pattern), in_specs...  27.5 us
    pallas_call x1, Pallas kernels, body(): pl.pallas_call(functools.partial(charge_kernel, count), grid=(chunks,), i...  11.7 us
    pallas_call x1, Pallas kernels, body(): pl.pallas_call(functools.partial(boundary_kernel, count), grid=(chunks,),...  7.69 us
    all_to_all x1, starting transfers between devices, body(): lax.all_to_all(copies, 'pencil', split_axis=0, concat_axis=0, tiled=True)  7.39 us
    sort x1, other arithmetic, body(): lax.sort((key.reshape(local_g), lax.iota(I32, local_g)), num_keys=1, is_s...  7.05 us
    pallas_call x1, Pallas kernels, body(): pl.pallas_call(functools.partial(last_kernel, count), in_specs=[smem()] +...  6.7 us
    all_to_all x1, starting transfers between devices, body(): lax.all_to_all(partial_raw, 'pencil', split_axis=0, concat_axis=0, tiled=...  6.01 us
    ppermute x3, starting transfers between devices, body(): lax.ppermute(sent, 'pencil', [(i, i ^ mask(i)) for i in range(count)])  4.45 us
  transfers between devices with their start and end apart: 8, of which 1 were waited for; matrix products, arithmetic and copies ran while one was open for 9% of the time, Pallas kernels for 40%

profile of v4, /device:TPU:0, one launch (start us, length us, event | category | flops | bytes accessed | tf_op | source)
XLA Modules:
  0.0 89.0 jit_solution(11282769986958382258)
XLA Ops:
  0.6 1.5 %atoms.1 = (f32[16,4,128]{2,1,0:T(4,128)}, s32[64,128]{1,0:T(8,128)}) custom-call(s32[1]{0:T(128)} %bitcast.place_ref.refs_0_, f32[4,81]{1,0:T(4,128)} %bitcast.33, f32[3,4]{1,0:T(4,128)} %positions_ref.1, s32[1,4]{1,0:T(1,128)} %bitcast.34, s32[64,128]{1,0:T(8,128)} %bitcast.26), custom_call_target="tpu_custom_call" | custom-call | tf_op jit(solution)/shard_map/atoms/pallas_call | solution.py:722
  2.2 7.4 %all-to-all-start = ((f32[16,4,128]{2,1,0:T(4,128)}), f32[16,4,128]{2,1,0:T(4,128)S(1)}, u32[]{:S(2)}, u32[]{:S(2)}) async-start(f32[16,4,128]{2,1,0:T(4,128)} %get-tuple-element.19), calls=%async_computation | async-start | bytes 65536 | tf_op jit(solution)/shard_map/all_to_all | solution.py:740
  9.6 7.0 %sort.15 = (s32[8192]{0:T(1024)}, s32[8192]{0:T(1024)}) sort(s32[8192]{0:T(1024)} %bitcast.32, s32[8192]{0:T(1024)S(1)} %iota.3), dimensions={0}, to_apply=%region_0.0 | sort | flops 106496 | bytes 131072 | tf_op jit(solution)/shard_map/sort | solution.py:743
  16.6 0.0 all-to-all-done
  16.6 0.0 copy-start.4
  16.6 0.6 copy-done.4
  17.2 11.7 %charge.1 = (f32[2,8192]{1,0:T(2,128)}, f32[200,128]{1,0:T(8,128)}, f32[64,8192]{1,0:T(8,128)}, f32[64,8192]{1,0:T(8,128)}) custom-call(s32[1]{0:T(128)} %bitcast.place_ref.refs_0_, f32[64,128]{1,0:T(8,128)} %bitcast.29, f32[3,128,256]{2,1,0:T(8,128)} %constant.17.clone.spread_ref, f32[8,128]{1,0:T(8,128)} %constant.16.clone.coef_ref, ...), custom_call_target="tpu_custom_call" | custom-call | flops 10000000000 | tf_op jit(solution)/shard_map/charge/pallas_call | solution.py:756
  28.9 3.8 %collective-permute-start.2 = (f32[200,128]{1,0:T(8,128)}, f32[200,128]{1,0:T(8,128)S(1)}, u32[]{:S(2)}, u32[]{:S(2)}) collective-permute-start(f32[200,128]{1,0:T(8,128)} %get-tuple-element.23), channel_id=1, source_target_pairs={{0,12},{1,15},{2,14},{3,13},{4,8},{5,11},{6,10},{7,9},{8,4},{9,7},... | collective-permute-start | bytes 307208 | tf_op jit(solution)/shard_map/ppermute | solution.py:826
  32.7 0.0 collective-permute-start.1
  32.7 0.7 collective-permute-start
  33.3 0.0 copy-start.3
  33.3 0.0 copy-start
  33.3 7.7 %boundary.1 = f32[64,128]{1,0:T(8,128)} custom-call(s32[1]{0:T(128)} %bitcast.place_ref.refs_0_, f32[64,128]{1,0:T(8,128)} %bitcast.30, f32[6,256,128]{2,1,0:T(8,128)} %constant.18.clone.gather_ref, f32[8,128]{1,0:T(8,128)} %constant.16.clone.coef_ref, s32[1,64]{1,0:T(1,128)} %bitcast.39, f32[9,3,8192]{2,1,0:T(4,128)} %bitcast.36, ...), custom_call_target="tpu_custom_call" | custom-call | flops 10000000000 | tf_op jit(solution)/shard_map/boundary/pallas_call | solution.py:794
  41.0 6.0 %all-to-all-start.1 = ((f32[16,4,128]{2,1,0:T(4,128)}), f32[16,4,128]{2,1,0:T(4,128)S(1)}, u32[]{:S(2)}, u32[]{:S(2)}) async-start(f32[16,4,128]{2,1,0:T(4,128)} %bitcast.31), calls=%async_computation.1 | async-start | bytes 65536 | tf_op jit(solution)/shard_map/all_to_all | solution.py:819
  47.0 0.0 collective-permute-done.2
  47.0 0.0 collective-permute-done.1
  47.0 0.0 collective-permute-done
  47.1 0.0 copy-done.3
  47.1 2.0 %collective-permute-start.3 = (f32[4,200,128]{2,1,0:T(8,128)S(1)}, f32[4,200,128]{2,1,0:T(8,128)S(1)}, u32[]{:S(2)}, u32[]{:S(2)}) collective-permute-start(f32[4,200,128]{2,1,0:T(8,128)S(1)} %pad_maximum_fusion.refs_1_), channel_id=1, source_target_pairs={{0,2},{1,3},{2,0},{3,1},{4,6},{5,7},{6,4},{7,5},{8,10},{9,11},{10,... | collective-permute-start | bytes 1228808 | tf_op jit(solution)/shard_map/ppermute | solution.py:831
  49.1 0.0 copy-done
  49.1 13.8 %planes_near.1 = (f32[2,2,640,128]{3,2,1,0:T(8,128)S(1)}, f32[2,2,640,128]{3,2,1,0:T(8,128)S(1)}) custom-call(s32[1]{0:T(128)} %bitcast.place_ref.refs_0_, f32[4,200,128]{2,1,0:T(8,128)S(1)} %pad_maximum_fusion.refs_1_, bf16[256,128]{1,0:T(8,128)(2,1)S(1)} %copy-done), custom_call_target="tpu_custom_call" | custom-call | flops 15000000512 | tf_op jit(solution)/shard_map/planes_near/pallas_call | solution.py:588
  62.9 0.0 copy-start.1
  62.9 1.1 %copy-done.1 = f32[2,2,640,128]{3,2,1,0:T(8,128)} copy-done((f32[2,2,640,128]{3,2,1,0:T(8,128)}, f32[2,2,640,128]{3,2,1,0:T(8,128)S(1)}, u32[]{:S(2)}) %copy-start.1) | copy-done | bytes 1310744
  64.0 0.0 collective-permute-start.4
  64.0 0.0 all-to-all-done.1
  64.0 0.0 collective-permute-done.3.refs_1_
  64.0 13.7 %planes_far.1 = (f32[2,2,640,128]{3,2,1,0:T(8,128)S(1)}, f32[2,2,640,128]{3,2,1,0:T(8,128)S(1)}) custom-call(s32[1]{0:T(128)} %bitcast.place_ref.refs_0_, f32[4,200,128]{2,1,0:T(8,128)S(1)} %collective-permute-done.3.refs_1_, bf16[256,128]{1,0:T(8,128)(2,1)S(1)} %copy-done), custom_call_target="tpu_custom_call" | custom-call | flops 15000000512 | tf_op jit(solution)/shard_map/planes_far/pallas_call | solution.py:588
  77.7 0.0 copy-start.2
  77.7 1.0 %copy-done.2 = f32[2,2,640,128]{3,2,1,0:T(8,128)} copy-done((f32[2,2,640,128]{3,2,1,0:T(8,128)}, f32[2,2,640,128]{3,2,1,0:T(8,128)S(1)}, u32[]{:S(2)}) %copy-start.2) | copy-done | bytes 1310744
  78.8 0.5 collective-permute-start.5
  79.3 0.6 slice_bitcast_fusion
  79.9 0.0 collective-permute-done.4.refs_2_
  79.9 2.2 %collective-permute-done.5.refs_3_ = f32[2,2,640,128]{3,2,1,0:T(8,128)} collective-permute-done((f32[2,2,640,128]{3,2,1,0:T(8,128)S(1)}, f32[2,2,640,128]{3,2,1,0:T(8,128)}, u32[]{:S(2)}, u32[]{:S(2)}) %collective-permute-start.5) | collective-permute-done | bytes 1310752 | tf_op jit(solution)/shard_map/ppermute | solution.py:836
  82.1 6.7 %last.1 = f32[4096,256]{1,0:T(8,128)} custom-call(s32[1]{0:T(128)} %bitcast.place_ref.refs_0_, f32[4,64,256]{2,1,0:T(8,128)} %constant.20.clone.wave_ref, f32[2,2,640,128]{3,2,1,0:T(8,128)} %copy-done.1, f32[2,2,640,128]{3,2,1,0:T(8,128)} %copy-done.2, f32[2,2,640,128]{3,2,1,0:T(8,128)} %collective-permute-done.4.refs_2_, ...), custom_call_target="tpu_custom_call" | custom-call | flops 7000000000 | tf_op jit(solution)/shard_map/last/pallas_call | solution.py:847
  (3 shorter events, 0.1 us)
Async XLA Ops:
  2.2 14.5 %all-to-all-start = ((f32[16,4,128]{2,1,0:T(4,128)}), f32[16,4,128]{2,1,0:T(4,128)S(1)}, u32[]{:S(2)}, u32[]{:S(2)}) async-start(f32[16,4,128]{2,1,0:T(4,128)} %get-tuple-element.19), calls=%async_computation | async-start | bytes 65536 | tf_op jit(solution)/shard_map/all_to_all | solution.py:740
  16.6 0.6 copy-start.4
  28.9 18.2 %collective-permute-start.2 = (f32[200,128]{1,0:T(8,128)}, f32[200,128]{1,0:T(8,128)S(1)}, u32[]{:S(2)}, u32[]{:S(2)}) collective-permute-start(f32[200,128]{1,0:T(8,128)} %get-tuple-element.23), channel_id=1, source_target_pairs={{0,12},{1,15},{2,14},{3,13},{4,8},{5,11},{6,10},{7,9},{8,4},{9,7},... | collective-permute-start | bytes 307208 | tf_op jit(solution)/shard_map/ppermute | solution.py:826
  32.7 14.4 %collective-permute-start.1 = (f32[200,128]{1,0:T(8,128)}, f32[200,128]{1,0:T(8,128)S(1)}, u32[]{:S(2)}, u32[]{:S(2)}) collective-permute-start(f32[200,128]{1,0:T(8,128)} %get-tuple-element.23), channel_id=1, source_target_pairs={{0,8},{1,9},{2,10},{3,11},{4,12},{5,13},{6,14},{7,15},{8,0},{9,1},... | collective-permute-start | bytes 307208 | tf_op jit(solution)/shard_map/ppermute | solution.py:826
  32.7 14.4 %collective-permute-start = (f32[200,128]{1,0:T(8,128)}, f32[200,128]{1,0:T(8,128)S(1)}, u32[]{:S(2)}, u32[]{:S(2)}) collective-permute-start(f32[200,128]{1,0:T(8,128)} %get-tuple-element.23), channel_id=1, source_target_pairs={{0,4},{1,7},{2,6},{3,5},{4,0},{5,3},{6,2},{7,1},{8,12},{9,15},{10,... | collective-permute-start | bytes 307208 | tf_op jit(solution)/shard_map/ppermute | solution.py:826
  33.3 13.7 %copy-start.3 = (f32[200,128]{1,0:T(8,128)S(1)}, f32[200,128]{1,0:T(8,128)}, u32[]{:S(2)}) copy-start(f32[200,128]{1,0:T(8,128)} %get-tuple-element.23) | copy-start | bytes 307204
  33.3 15.8 %copy-start = (bf16[256,128]{1,0:T(8,128)(2,1)S(1)}, bf16[256,128]{1,0:T(8,128)(2,1)}, u32[]{:S(2)}) copy-start(bf16[256,128]{1,0:T(8,128)(2,1)} %constant.19.clone.refs_2_) | copy-start | bytes 196612
  41.0 23.0 %all-to-all-start.1 = ((f32[16,4,128]{2,1,0:T(4,128)}), f32[16,4,128]{2,1,0:T(4,128)S(1)}, u32[]{:S(2)}, u32[]{:S(2)}) async-start(f32[16,4,128]{2,1,0:T(4,128)} %bitcast.31), calls=%async_computation.1 | async-start | bytes 65536 | tf_op jit(solution)/shard_map/all_to_all | solution.py:819
  47.1 16.9 %collective-permute-start.3 = (f32[4,200,128]{2,1,0:T(8,128)S(1)}, f32[4,200,128]{2,1,0:T(8,128)S(1)}, u32[]{:S(2)}, u32[]{:S(2)}) collective-permute-start(f32[4,200,128]{2,1,0:T(8,128)S(1)} %pad_maximum_fusion.refs_1_), channel_id=1, source_target_pairs={{0,2},{1,3},{2,0},{3,1},{4,6},{5,7},{6,4},{7,5},{8,10},{9,11},{10,... | collective-permute-start | bytes 1228808 | tf_op jit(solution)/shard_map/ppermute | solution.py:831
  62.9 1.1 %copy-start.1 = (f32[2,2,640,128]{3,2,1,0:T(8,128)}, f32[2,2,640,128]{3,2,1,0:T(8,128)S(1)}, u32[]{:S(2)}) copy-start(f32[2,2,640,128]{3,2,1,0:T(8,128)S(1)} %get-tuple-element.30.refs_0_) | copy-start | bytes 3932164
  64.0 15.9 %collective-permute-start.4 = (f32[2,2,640,128]{3,2,1,0:T(8,128)S(1)}, f32[2,2,640,128]{3,2,1,0:T(8,128)}, u32[]{:S(2)}, u32[]{:S(2)}) collective-permute-start(f32[2,2,640,128]{3,2,1,0:T(8,128)S(1)} %get-tuple-element.33), channel_id=1, source_target_pairs={{0,1},{1,0},{2,3},{3,2},{4,5},{5,4},{6,7},{7,6},{8,9},{9,8},{10,11... | collective-permute-start | bytes 3932168 | tf_op jit(solution)/shard_map/ppermute | solution.py:833
  77.7 1.1 %copy-start.2 = (f32[2,2,640,128]{3,2,1,0:T(8,128)}, f32[2,2,640,128]{3,2,1,0:T(8,128)S(1)}, u32[]{:S(2)}) copy-start(f32[2,2,640,128]{3,2,1,0:T(8,128)S(1)} %get-tuple-element.32.refs_1_) | copy-start | bytes 3932164
  78.8 3.3 %collective-permute-start.5 = (f32[2,2,640,128]{3,2,1,0:T(8,128)S(1)}, f32[2,2,640,128]{3,2,1,0:T(8,128)}, u32[]{:S(2)}, u32[]{:S(2)}) collective-permute-start(f32[2,2,640,128]{3,2,1,0:T(8,128)S(1)} %get-tuple-element.34), channel_id=1, source_target_pairs={{0,1},{1,0},{2,3},{3,2},{4,5},{5,4},{6,7},{7,6},{8,9},{9,8},{10,11... | collective-permute-start | bytes 3932168 | tf_op jit(solution)/shard_map/ppermute | solution.py:836
